TPU v7x, 256 devices: a whole 4x4x8 slice. The times are simulated.
256 devices in a mesh: pipe: 4 (over y_lo, core), expert: 64 (over x, z, y_hi).
Axes of the slice: x: 4, y: 4 (y_hi: 2, y_lo: 2; y = y_hi * 2 + y_lo), z: 8, core: 2. Of those that a mesh axis runs over, the one named last changes fastest.
Arguments:
- tokens: bfloat16 [32768, 3584], P(('pipe', 'expert')), may hold values from -6 to 6
- expert_ids: int32 [32768, 8], P(('pipe', 'expert')), may hold values from 0 to 255, all different within a row; in each aligned block of 128 rows (0 to 127, 128 to 255, ...) at most 8 rows name the same one
- gate_values: bfloat16 [32768, 8], P(('pipe', 'expert')), may hold values from 0.25 to 2.5
- cotangent: bfloat16 [32768, 3584], P(('pipe', 'expert')), may hold values from -0.1796875 to 0.1796875
- w_gate: bfloat16 [3584, 16384], P(None, 'expert'), may hold values from -0.09375 to 0.09375
- w_up: bfloat16 [3584, 16384], P(None, 'expert'), may hold values from -0.09375 to 0.09375
- w_down: bfloat16 [16384, 3584], P('expert'), may hold values from -0.125 to 0.125
Outputs:
- mixed: bfloat16 [32768, 3584], P(('pipe', 'expert'))
- gate_grad: float32 [32768, 8], P(('pipe', 'expert'))
- grad_gate: bfloat16 [4, 3584, 16384], P('pipe', None, 'expert')
- grad_up: bfloat16 [4, 3584, 16384], P('pipe', None, 'expert')
Inputs may be any that keep to these rules, and one draw needn't show every extreme that they name: `expert_ids`: each row names 8 different experts; within the rows of one device no expert is named by more than 8 rows, a bound that some block reaches.
All inputs are finite; a program needn't handle non-finite values.
Results may differ from a plain program's by a relative error of at most 0.02.
Values may be sent and summed in bfloat16 or wider, within the bound.
A program may use at most 128 MiB of HBM per device.

v0:
```python
import jax
import jax.numpy as jnp
from jax import lax
from jax.sharding import PartitionSpec as P

FFW = 2048
CAP = 8


def from_partner(shard, axis, stride):
    return lax.ppermute(shard, axis, [(i, i ^ 1 << stride) for i in range(lax.axis_size(axis))])


def slot_tables(expert_ids, gate_values, flight_count, capacity):
    experts = jnp.arange(flight_count, dtype=jnp.int32)
    match = (expert_ids[:, :, None] == experts[None, None, :]).astype(jnp.float32)
    counted = jnp.sum(match, axis=1)
    before = jnp.cumsum(counted, axis=0) - counted
    places = jnp.arange(capacity, dtype=jnp.float32)
    slot_hit = counted[:, :, None] * (before[:, :, None] == places[None, None, :]).astype(
        jnp.float32
    )
    gate_each = jnp.sum(match * gate_values.astype(jnp.float32)[:, :, None], axis=1)
    return (match, slot_hit, gate_each)


def per_device(tokens, expert_ids, gate_values, cotangent, w_gate, w_up, w_down):
    device_count = lax.axis_size("expert")
    hidden_dev = w_gate.shape[1]
    slice_count = FFW // hidden_dev
    flight_count = device_count // slice_count
    model_width = tokens.shape[1]
    capacity = CAP
    row_contract = (((0,), (0,)), ((), ()))
    match, slot_hit, gate_each = slot_tables(expert_ids, gate_values, flight_count, capacity)
    hit_flat = slot_hit.reshape(slot_hit.shape[0], flight_count * capacity).astype(jnp.bfloat16)
    token_buf = lax.dot_general(
        hit_flat, tokens, row_contract, preferred_element_type=jnp.float32
    ).astype(jnp.bfloat16)
    cot_buf = lax.dot_general(
        hit_flat, cotangent, row_contract, preferred_element_type=jnp.float32
    ).astype(jnp.bfloat16)
    gate_buf = jnp.sum(slot_hit * gate_each[:, :, None], axis=0).astype(jnp.bfloat16)
    token_buf = token_buf.reshape(flight_count, capacity, model_width)
    cot_buf = cot_buf.reshape(flight_count, capacity, model_width)
    send_tokens = jnp.repeat(token_buf, slice_count, axis=0)
    send_cots = jnp.repeat(cot_buf, slice_count, axis=0)
    send_gates = jnp.repeat(gate_buf, slice_count, axis=0)
    recv_tokens, recv_cots, recv_gates = (
        lax.all_to_all(send_tokens, "expert", split_axis=0, concat_axis=0, tiled=True),
        lax.all_to_all(send_cots, "expert", split_axis=0, concat_axis=0, tiled=True),
        lax.all_to_all(send_gates, "expert", split_axis=0, concat_axis=0, tiled=True),
    )
    token_rows = recv_tokens.reshape(device_count * capacity, model_width)
    cot_rows = recv_cots.reshape(device_count * capacity, model_width)
    pre_gate = jnp.dot(token_rows, w_gate, preferred_element_type=jnp.float32)
    pre_up = jnp.dot(token_rows, w_up, preferred_element_type=jnp.float32)
    sigmoid_gate = jax.nn.sigmoid(pre_gate)
    hidden = (pre_gate * sigmoid_gate * pre_up).astype(jnp.bfloat16)
    partial_out = jnp.dot(hidden, w_down, preferred_element_type=jnp.float32).astype(jnp.bfloat16)
    returned = lax.all_to_all(
        partial_out.reshape(device_count, capacity, model_width),
        "expert",
        split_axis=0,
        concat_axis=0,
        tiled=True,
    )
    grouped = returned.reshape(flight_count, slice_count, capacity, model_width)
    weight_hit = (slot_hit * gate_each[:, :, None]).astype(jnp.bfloat16)
    mixed = jnp.einsum(
        "tec,escd->td", weight_hit, grouped, preferred_element_type=jnp.float32
    ).astype(jnp.bfloat16)
    values = jnp.einsum("escd,ecd->ec", grouped, cot_buf, preferred_element_type=jnp.float32)
    value_each = jnp.einsum("tec,ec->te", slot_hit, values)
    gate_grad = jnp.einsum("tke,te->tk", match, value_each)
    scaled = (recv_gates.reshape(-1, 1).astype(jnp.float32) * cot_rows.astype(jnp.float32)).astype(
        jnp.bfloat16
    )
    back_hidden = lax.dot_general(
        scaled, w_down, (((1,), (1,)), ((), ())), preferred_element_type=jnp.float32
    )
    d_up = (back_hidden * pre_gate * sigmoid_gate).astype(jnp.bfloat16)
    d_pre = (back_hidden * pre_up * sigmoid_gate * (1.0 + pre_gate * (1.0 - sigmoid_gate))).astype(
        jnp.bfloat16
    )
    term_gate = lax.dot_general(
        token_rows, d_pre, row_contract, preferred_element_type=jnp.float32
    ).astype(jnp.bfloat16)
    term_up = lax.dot_general(
        token_rows, d_up, row_contract, preferred_element_type=jnp.float32
    ).astype(jnp.bfloat16)
    mirrored = (term_gate, term_up)
    for bit_number in range(lax.axis_size("pipe").bit_length() - 1):
        mirrored = from_partner((mirrored[0], mirrored[1]), "pipe", bit_number)
    grad_gate = (term_gate.astype(jnp.float32) + mirrored[0].astype(jnp.float32)).astype(
        jnp.bfloat16
    )[None]
    grad_up = (term_up.astype(jnp.float32) + mirrored[1].astype(jnp.float32)).astype(jnp.bfloat16)[
        None
    ]
    return (mixed, gate_grad, grad_gate, grad_up)


def solution(mesh):
    placed = (
        P(("pipe", "expert"), None),
        P(("pipe", "expert"), None),
        P(("pipe", "expert"), None),
        P(("pipe", "expert"), None),
        P(None, "expert"),
        P(None, "expert"),
        P("expert", None),
    )
    return jax.shard_map(
        per_device,
        mesh=mesh,
        in_specs=placed,
        out_specs=(
            P(("pipe", "expert"), None),
            P(("pipe", "expert"), None),
            P("pipe", None, "expert"),
            P("pipe", None, "expert"),
        ),
        check_vma=False,
    )
```

profile of v0, /device:TPU:1, one launch (start us, length us, event | category | flops | bytes accessed | tf_op | source)
XLA Modules:
  0.0 407.9 jit_solution(10472979008175689330)
XLA Ops:
  0.6 0.0 copy-start
  0.6 0.8 convert_element_type.89
  1.5 0.1 eq.45
  1.6 0.7 select_reduce_fusion.1
  2.3 0.1 copy.23
  2.4 0.2 reduce_window_sum.11
  2.6 1.5 fusion.3
  4.1 0.3 broadcast_in_dim.10
  4.4 0.0 copy-start.4
  4.4 99.8 %all_to_all.24 = bf16[64,8,3584]{2,1,0:T(8,128)(2,1)S(1)} all-to-all(bf16[64,8,3584]{2,1,0:T(8,128)(2,1)S(1)} %bitcast.72), channel_id=1, replica_groups=mesh['pipe'=4,'expert'=64] {'expert'}, dimensions={0} | all-to-all | bytes 7340032 | tf_op jit(solution)/shard_map/all_to_all | solution.py:50
  104.2 1.1 fusion.12
  105.4 0.8 copy-done.1
  106.1 1.0 copy-done.5
  107.1 1.1 fusion.10
  108.2 0.8 copy-done.8
  109.0 3.0 fusion.1
  112.0 7.3 %all-to-all-start.1 = ((bf16[64,8,3584]{2,1,0:T(8,128)(2,1)}), bf16[64,8,3584]{2,1,0:T(8,128)(2,1)}, u32[]{:S(2)}, u32[]{:S(2)}) async-start(bf16[64,8,3584]{2,1,0:T(8,128)(2,1)} %fusion.1), calls=%async_computation.1 | async-start | bytes 7340032 | tf_op jit(solution)/shard_map/all_to_all | solution.py:61
  119.3 0.1 fusion.22
  119.4 0.1 copy.26
  119.5 0.1 broadcast_in_dim.11
  119.6 0.1 all_to_all.17
  119.7 0.7 copy.27
  120.4 82.2 %all-to-all-done.1 = bf16[64,8,3584]{2,1,0:T(8,128)(2,1)} async-done(((bf16[64,8,3584]{2,1,0:T(8,128)(2,1)}), bf16[64,8,3584]{2,1,0:T(8,128)(2,1)}, u32[]{:S(2)}, u32[]{:S(2)}) %all-to-all-start.1) | async-done | bytes 3670048 | tf_op jit(solution)/shard_map/all_to_all | solution.py:61
  202.6 8.5 %all-to-all-start.2 = ((bf16[64,1,8]{2,1,0:T(2,128)(2,1)}), bf16[64,1,8]{2,1,0:T(2,128)(2,1)S(1)}, u32[]{:S(2)}, u32[]{:S(2)}) async-start(bf16[64,1,8]{2,1,0:T(2,128)(2,1)} %copy.27), calls=%async_computation.2 | async-start | bytes 65536 | tf_op jit(solution)/shard_map/all_to_all | solution.py:52
  211.1 2.6 convert_reduce_fusion
  213.8 1.6 multiply_reduce_fusion
  215.4 6.4 %all-to-all-done.2 = bf16[64,1,8]{2,1,0:T(2,128)(2,1)S(1)} async-done(((bf16[64,1,8]{2,1,0:T(2,128)(2,1)}), bf16[64,1,8]{2,1,0:T(2,128)(2,1)S(1)}, u32[]{:S(2)}, u32[]{:S(2)}) %all-to-all-start.2) | async-done | bytes 1056 | tf_op jit(solution)/shard_map/all_to_all | solution.py:52
  221.8 2.2 broadcast_in_dim.12
  223.9 6.0 %all-to-all-start.3 = ((bf16[64,8,3584]{2,1,0:T(8,128)(2,1)}), bf16[64,8,3584]{2,1,0:T(8,128)(2,1)}, u32[]{:S(2)}, u32[]{:S(2)}) async-start(bf16[64,8,3584]{2,1,0:T(8,128)(2,1)} %bitcast.71), calls=%async_computation.3 | async-start | bytes 7340032 | tf_op jit(solution)/shard_map/all_to_all | solution.py:51
  230.0 0.1 convert_reduce_fusion.1
  230.1 0.1 reshape.71
  230.1 83.3 %all-to-all-done.3 = bf16[64,8,3584]{2,1,0:T(8,128)(2,1)} async-done(((bf16[64,8,3584]{2,1,0:T(8,128)(2,1)}), bf16[64,8,3584]{2,1,0:T(8,128)(2,1)}, u32[]{:S(2)}, u32[]{:S(2)}) %all-to-all-start.3) | async-done | bytes 3670048 | tf_op jit(solution)/shard_map/all_to_all | solution.py:51
  313.5 3.3 fusion.5
  316.9 1.3 convolution_convert_fusion.1
  318.2 4.0 collective-permute-start.2
  322.2 1.4 convolution_convert_fusion.2
  323.6 0.1 collective-permute-start
  323.7 1.9 collective-permute-done.2
  325.6 0.4 collective-permute-start.3
  326.0 2.2 collective-permute-done
  328.2 0.4 collective-permute-start.1
  328.6 0.1 fusion.20
  328.7 0.6 select_reduce_fusion
  329.3 1.4 fusion.2
  330.7 36.1 %collective-permute-done.3 = bf16[3584,256]{1,0:T(8,128)(2,1)S(1)} collective-permute-done((bf16[3584,256]{1,0:T(8,128)(2,1)S(1)}, bf16[3584,256]{1,0:T(8,128)(2,1)S(1)}, u32[]{:S(2)}, u32[]{:S(2)}) %collective-permute-start.3) | collective-permute-done | bytes 1835040 | tf_op jit(solution)/shard_map/ppermute | solution.py:11
  366.8 1.8 fusion.16
  368.6 37.6 %collective-permute-done.1 = bf16[3584,256]{1,0:T(8,128)(2,1)S(1)} collective-permute-done((bf16[3584,256]{1,0:T(8,128)(2,1)S(1)}, bf16[3584,256]{1,0:T(8,128)(2,1)S(1)}, u32[]{:S(2)}, u32[]{:S(2)}) %collective-permute-start.1) | collective-permute-done | bytes 1835040 | tf_op jit(solution)/shard_map/ppermute | solution.py:11
  406.1 1.8 fusion.15
  (18 shorter events, 0.1 us)
Async XLA Ops:
  0.6 108.4 %copy-start = (bf16[256,3584]{1,0:T(8,128)(2,1)S(1)}, bf16[256,3584]{1,0:T(8,128)(2,1)}, u32[]{:S(2)}) copy-start(bf16[256,3584]{1,0:T(8,128)(2,1)} %param.13) | copy-start | bytes 5505028
  4.4 99.9 %copy-start.4 = (bf16[3584,256]{1,0:T(8,128)(2,1)S(1)}, bf16[3584,256]{1,0:T(8,128)(2,1)}, u32[]{:S(2)}) copy-start(bf16[3584,256]{1,0:T(8,128)(2,1)} %param.11) | copy-start | bytes 5505028
  104.2 1.9 copy-start.1
  104.2 2.8 copy-start.5
  107.1 1.1 copy-start.6
  108.2 0.8 copy-start.8
  112.0 90.6 %all-to-all-start.1 = ((bf16[64,8,3584]{2,1,0:T(8,128)(2,1)}), bf16[64,8,3584]{2,1,0:T(8,128)(2,1)}, u32[]{:S(2)}, u32[]{:S(2)}) async-start(bf16[64,8,3584]{2,1,0:T(8,128)(2,1)} %fusion.1), calls=%async_computation.1 | async-start | bytes 7340032 | tf_op jit(solution)/shard_map/all_to_all | solution.py:61
  202.6 19.2 %all-to-all-start.2 = ((bf16[64,1,8]{2,1,0:T(2,128)(2,1)}), bf16[64,1,8]{2,1,0:T(2,128)(2,1)S(1)}, u32[]{:S(2)}, u32[]{:S(2)}) async-start(bf16[64,1,8]{2,1,0:T(2,128)(2,1)} %copy.27), calls=%async_computation.2 | async-start | bytes 65536 | tf_op jit(solution)/shard_map/all_to_all | solution.py:52
  223.9 89.5 %all-to-all-start.3 = ((bf16[64,8,3584]{2,1,0:T(8,128)(2,1)}), bf16[64,8,3584]{2,1,0:T(8,128)(2,1)}, u32[]{:S(2)}, u32[]{:S(2)}) async-start(bf16[64,8,3584]{2,1,0:T(8,128)(2,1)} %bitcast.71), calls=%async_computation.3 | async-start | bytes 7340032 | tf_op jit(solution)/shard_map/all_to_all | solution.py:51
  313.5 3.4 copy-start.2
  313.5 3.4 copy-start.7
  316.8 5.3 %copy-start.9 = (f32[512,256]{1,0:T(8,128)S(1)}, f32[512,256]{1,0:T(8,128)}, u32[]{:S(2)}) copy-start(f32[512,256]{1,0:T(8,128)} %copy-done.8) | copy-start | bytes 1572868
  318.2 10.5 %copy-start.3 = (s32[128,8]{0,1:T(8,128)S(1)}, s32[128,8]{0,1:T(8,128)}, u32[]{:S(2)}) copy-start(s32[128,8]{0,1:T(8,128)} %param.8) | copy-start | bytes 12292
  318.2 7.4 %collective-permute-start.2 = (bf16[3584,256]{1,0:T(8,128)(2,1)S(1)}, bf16[3584,256]{1,0:T(8,128)(2,1)S(1)}, u32[]{:S(2)}, u32[]{:S(2)}) collective-permute-start(bf16[3584,256]{1,0:T(8,128)(2,1)S(1)} %convolution_convert_fusion.1), channel_id=1, source_target_pairs={{0,64},{64,0},{128,192},{192,128},{1,65},{65,1},{129,193},{193,129... | collective-permute-start | bytes 5505032 | tf_op jit(solution)/shard_map/ppermute | solution.py:11
  323.6 4.6 %collective-permute-start = (bf16[3584,256]{1,0:T(8,128)(2,1)S(1)}, bf16[3584,256]{1,0:T(8,128)(2,1)S(1)}, u32[]{:S(2)}, u32[]{:S(2)}) collective-permute-start(bf16[3584,256]{1,0:T(8,128)(2,1)S(1)} %convolution_convert_fusion.2), channel_id=1, source_target_pairs={{0,64},{64,0},{128,192},{192,128},{1,65},{65,1},{129,193},{193,129... | collective-permute-start | bytes 5505032 | tf_op jit(solution)/shard_map/ppermute | solution.py:11
  325.6 41.2 %collective-permute-start.3 = (bf16[3584,256]{1,0:T(8,128)(2,1)S(1)}, bf16[3584,256]{1,0:T(8,128)(2,1)S(1)}, u32[]{:S(2)}, u32[]{:S(2)}) collective-permute-start(bf16[3584,256]{1,0:T(8,128)(2,1)S(1)} %collective-permute-done.2), channel_id=1, source_target_pairs={{0,128},{64,192},{128,0},{192,64},{1,129},{65,193},{129,1},{193,65... | collective-permute-start | bytes 5505032 | tf_op jit(solution)/shard_map/ppermute | solution.py:11
  328.2 77.9 %collective-permute-start.1 = (bf16[3584,256]{1,0:T(8,128)(2,1)S(1)}, bf16[3584,256]{1,0:T(8,128)(2,1)S(1)}, u32[]{:S(2)}, u32[]{:S(2)}) collective-permute-start(bf16[3584,256]{1,0:T(8,128)(2,1)S(1)} %collective-permute-done), channel_id=1, source_target_pairs={{0,128},{64,192},{128,0},{192,64},{1,129},{65,193},{129,1},{193,65... | collective-permute-start | bytes 5505032 | tf_op jit(solution)/shard_map/ppermute | solution.py:11
where the time goes:
time: 408 us
  waiting for transfers between devices  250 us (61%)
  blocking collectives  99.8 us (24%)
  starting transfers between devices  26.7 us (7%)
  matrix products  15.9 us (4%)
  other arithmetic  8.65 us (2%)
  local copies, waits for them, and re-layouts  6.27 us (2%)
    all_to_all x1, blocking collectives, per_device(): lax.all_to_all(send_tokens, 'expert', split_axis=0, concat_axis=0, tiled=...  99.8 us
    all_to_all x1, waiting for transfers between devices, per_device(): lax.all_to_all(send_cots, 'expert', split_axis=0, concat_axis=0, tiled=True)  83.3 us
    all_to_all x1, waiting for transfers between devices, per_device(): lax.all_to_all(partial_out.reshape(device_count, capacity, model_width),...  82.2 us
    ppermute x4, waiting for transfers between devices, from_partner(): lax.ppermute(shard, axis, [(i, i ^ 1 << stride) for i in range(lax.axis_s...  77.8 us
    all_to_all x1, starting transfers between devices, per_device(): lax.all_to_all(send_gates, 'expert', split_axis=0, concat_axis=0, tiled=T...  8.52 us
  transfers between devices with their start and end apart: 7, of which 7 were waited for; matrix products, arithmetic and copies ran while one was open for 3% of the time, Pallas kernels for 0%

commit v1 on v0

v1 whole, which is shorter than its diff:
```python
import jax
import jax.numpy as jnp
from jax import lax
from jax.experimental import pallas as pl
from jax.experimental.pallas import tpu as pltpu
from jax.sharding import PartitionSpec as P

FFW = 2048
CAP = 8
MESH = pl.DeviceIdType.MESH
NX, NZ, NY = 4, 8, 4
PLANE = NX * NZ
GRP = 4
NG = PLANE // GRP


def where_am_i():
    p, i = lax.axis_index("pipe"), lax.axis_index("expert")
    x, z, y_hi = i // (2 * NZ), (i // 2) % NZ, i % 2
    return p, x, 2 * y_hi + p // 2, z, p % 2


def device_at(x, y, z, core):
    return ((y % 2) * 2 + core, (x * NZ + z) * 2 + y // 2)


def offset_of(k):
    return k // NZ, k % NZ


def ahead(x, z, k):
    dx, dz = offset_of(k)
    return (x + dx) % NX, (z + dz) % NZ


def behind(x, z, k):
    dx, dz = offset_of(k)
    return (x + NX - dx) % NX, (z + NZ - dz) % NZ


def greet_plane(barrier, x, y, z, core):
    def greet(k, carry):
        xd, zd = ahead(x, z, k)
        pl.semaphore_signal(
            barrier, inc=1, device_id=device_at(xd, y, zd, core), device_id_type=MESH
        )
        return carry

    lax.fori_loop(1, PLANE, greet, 0)


def dispatch_kernel(
    send_x, send_c, out_x, out_c, stage, plane_send, plane_recv, y_send, y_recv
):
    p, x, y, z, core = where_am_i()
    up, down, across = (y + 1) % NY, (y + NY - 1) % NY, (y + 2) % NY
    barrier = pltpu.get_barrier_semaphore()
    greet_plane(barrier, x, y, z, core)

    @pl.when(core == 0)
    def _():
        pl.semaphore_signal(
            barrier, inc=1, device_id=device_at(x, across, z, core), device_id_type=MESH
        )
        pl.semaphore_wait(barrier, PLANE)

    @pl.when(core == 1)
    def _():
        for to in (up, down):
            pl.semaphore_signal(
                barrier, inc=1, device_id=device_at(x, to, z, core), device_id_type=MESH
            )
        pl.semaphore_wait(barrier, PLANE + 1)

    sends = (send_x, send_c)
    outs = (out_x, out_c)

    def plane_copy(a, k):
        xd, zd = ahead(x, z, k)
        return pltpu.make_async_remote_copy(
            src_ref=sends[a].at[xd * 2 + zd // 4],
            dst_ref=stage.at[a, k],
            send_sem=plane_send.at[a, k],
            recv_sem=plane_recv.at[a, k],
            device_id=device_at(xd, y, zd, core),
            device_id_type=MESH,
        )

    def own_copy(a):
        return pltpu.make_async_copy(
            sends[a].at[x * 2 + z // 4], stage.at[a, 0], plane_recv.at[a, 0]
        )

    def y_copy(a, g, half, to):
        rows = pl.ds(g * GRP, GRP)
        return pltpu.make_async_remote_copy(
            src_ref=stage.at[a, rows],
            dst_ref=outs[a].at[pl.ds(half * PLANE + g * GRP, GRP)],
            send_sem=y_send.at[a, half, g],
            recv_sem=y_recv.at[a, half, g],
            device_id=device_at(x, to, z, core),
            device_id_type=MESH,
        )

    def keep_copy(a, g):
        rows = pl.ds(g * GRP, GRP)
        return pltpu.make_async_copy(stage.at[a, rows], outs[a].at[rows], y_recv.at[a, 0, g])

    for a in range(2):
        own_copy(a).start()

        def start(k, carry, a=a):
            plane_copy(a, k).start()
            return carry

        lax.fori_loop(1, PLANE, start, 0)

    for a in range(2):
        own_copy(a).wait()

        def forward(g, carry, a=a):
            def arrived(k, inner):
                plane_copy(a, k).wait_recv()
                return inner

            lax.fori_loop(jnp.maximum(g * GRP, 1), g * GRP + GRP, arrived, 0)

            @pl.when(core == 0)
            def _():
                y_copy(a, g, 1, across).start()
                keep_copy(a, g).start()

            @pl.when(core == 1)
            def _():
                y_copy(a, g, 0, up).start()
                y_copy(a, g, 1, down).start()

            return carry

        lax.fori_loop(0, NG, forward, 0)

    for a in range(2):

        def finish_plane(k, carry, a=a):
            plane_copy(a, k).wait_send()
            return carry

        lax.fori_loop(1, PLANE, finish_plane, 0)

        def finish(g, carry, a=a):
            @pl.when(core == 0)
            def _():
                y_copy(a, g, 1, across).wait()
                keep_copy(a, g).wait()

            @pl.when(core == 1)
            def _():
                y_copy(a, g, 0, up).wait()
                y_copy(a, g, 1, down).wait()

            return carry

        lax.fori_loop(0, NG, finish, 0)


def return_kernel(
    part,
    terms,
    out_rows,
    out_gate,
    out_up,
    landed,
    summed,
    theirs,
    total,
    plane_send,
    plane_recv,
    y_send,
    y_recv,
    core_send,
    core_recv,
    sum_send,
    sum_recv,
    keep_sem,
):
    p, x, y, z, core = where_am_i()
    up, down, across = (y + 1) % NY, (y + NY - 1) % NY, (y + 2) % NY
    partner = y + 1 - 2 * (y % 2)
    half_rows = terms.shape[0] // 2
    barrier = pltpu.get_barrier_semaphore()
    greet_plane(barrier, x, y, z, core)

    def greet(to_y, to_core):
        pl.semaphore_signal(
            barrier, inc=1, device_id=device_at(x, to_y, z, to_core), device_id_type=MESH
        )

    @pl.when(core == 0)
    def _():
        greet(across, 0)
        greet(y, 1)

    @pl.when(core == 1)
    def _():
        greet(up, 1)
        greet(down, 1)
        greet(y, 0)
        greet(partner, 0)

    pl.semaphore_wait(barrier, PLANE + 2)

    def y_copy(g, half, to):
        return pltpu.make_async_remote_copy(
            src_ref=part.at[pl.ds(half * PLANE + g * GRP, GRP)],
            dst_ref=landed.at[half, pl.ds(g * GRP, GRP)],
            send_sem=y_send.at[half, g],
            recv_sem=y_recv.at[half, g],
            device_id=device_at(x, to, z, core),
            device_id_type=MESH,
        )

    def plane_copy(k):
        xd, zd = behind(x, z, k)
        return pltpu.make_async_remote_copy(
            src_ref=summed.at[k],
            dst_ref=out_rows.at[x * NZ + z],
            send_sem=plane_send.at[k],
            recv_sem=plane_recv.at[k],
            device_id=device_at(xd, y, zd, core),
            device_id_type=MESH,
        )

    def own_copy():
        return pltpu.make_async_copy(summed.at[0], out_rows.at[x * NZ + z], plane_recv.at[0])

    def core_copy():
        other = (1 - core) * half_rows
        return pltpu.make_async_remote_copy(
            src_ref=terms.at[pl.ds(other, half_rows)],
            dst_ref=theirs,
            send_sem=core_send,
            recv_sem=core_recv,
            device_id=device_at(x, y, z, 1 - core),
            device_id_type=MESH,
        )

    outs = (out_gate, out_up)

    def sum_copy(w, half, to_y, to_core):
        return pltpu.make_async_remote_copy(
            src_ref=total.at[w],
            dst_ref=outs[w].at[pl.ds(half * half_rows, half_rows)],
            send_sem=sum_send.at[w, to_core],
            recv_sem=sum_recv.at[w, half],
            device_id=device_at(x, to_y, z, to_core),
            device_id_type=MESH,
        )

    def keep_copy(w):
        return pltpu.make_async_copy(
            total.at[w], outs[w].at[pl.ds(0, half_rows)], keep_sem.at[w]
        )

    core_copy().start()

    def start_y(g, carry):
        @pl.when(core == 0)
        def _():
            y_copy(g, 1, across).start()

        @pl.when(core == 1)
        def _():
            y_copy(g, 0, down).start()
            y_copy(g, 1, up).start()

        return carry

    lax.fori_loop(0, NG, start_y, 0)

    core_copy().wait()
    step = 16
    columns = total.shape[-1]

    def add_terms(t, carry):
        at = pl.ds(t * step, step)
        mine = terms[pl.ds(core * half_rows + t * step, step)].astype(jnp.float32)
        both = (mine + theirs[at].astype(jnp.float32)).astype(jnp.bfloat16)
        total[0, at] = both[:, :, :columns]
        total[1, at] = both[:, :, columns:]
        return carry

    lax.fori_loop(0, half_rows // step, add_terms, 0)

    @pl.when(core == 0)
    def _():
        for w in range(2):
            sum_copy(w, 0, partner, 1).start()
            keep_copy(w).start()

    @pl.when(core == 1)
    def _():
        for w in range(2):
            sum_copy(w, 1, partner, 1).start()
            sum_copy(w, 1, y, 0).start()

    def add_and_send(g, carry):
        @pl.when(core == 0)
        def _():
            y_copy(g, 1, across).wait()

            def add(b, inner):
                summed[b] = (
                    part[b].astype(jnp.float32) + landed[1, b].astype(jnp.float32)
                ).astype(jnp.bfloat16)
                return inner

            lax.fori_loop(g * GRP, g * GRP + GRP, add, 0)

        @pl.when(core == 1)
        def _():
            y_copy(g, 0, down).wait()
            y_copy(g, 1, up).wait()

            def add(b, inner):
                summed[b] = (
                    landed[0, b].astype(jnp.float32) + landed[1, b].astype(jnp.float32)
                ).astype(jnp.bfloat16)
                return inner

            lax.fori_loop(g * GRP, g * GRP + GRP, add, 0)

        def send(k, inner):
            plane_copy(k).start()
            return inner

        lax.fori_loop(jnp.maximum(g * GRP, 1), g * GRP + GRP, send, 0)
        return carry

    lax.fori_loop(0, NG, add_and_send, 0)
    own_copy().start()
    own_copy().wait()

    def finish(k, carry):
        plane_copy(k).wait()
        return carry

    lax.fori_loop(1, PLANE, finish, 0)

    @pl.when(core == 0)
    def _():
        for w in range(2):
            sum_copy(w, 0, partner, 1).wait_send()
            keep_copy(w).wait()
            sum_copy(w, 1, y, 0).wait_recv()

    @pl.when(core == 1)
    def _():
        for w in range(2):
            sum_copy(w, 1, partner, 1).wait()
            sum_copy(w, 1, y, 0).wait_send()
            sum_copy(w, 0, partner, 1).wait_recv()


def dispatch(send_x, send_c):
    block = send_x.shape[1:]
    landed = jax.ShapeDtypeStruct((2 * PLANE,) + block, jnp.bfloat16)
    return pl.pallas_call(
        dispatch_kernel,
        out_shape=(landed, landed),
        in_specs=[pl.BlockSpec(memory_space=pltpu.VMEM)] * 2,
        out_specs=[pl.BlockSpec(memory_space=pl.ANY)] * 2,
        scratch_shapes=[
            pltpu.VMEM((2, PLANE) + block, jnp.bfloat16),
            pltpu.SemaphoreType.DMA((2, PLANE)),
            pltpu.SemaphoreType.DMA((2, PLANE)),
            pltpu.SemaphoreType.DMA((2, 2, NG)),
            pltpu.SemaphoreType.DMA((2, 2, NG)),
        ],
        compiler_params=pltpu.CompilerParams(
            collective_id=0, has_side_effects=True, vmem_limit_bytes=24 << 20
        ),
    )(send_x, send_c)


def give_back(part, terms):
    block = part.shape[1:]
    blocks, rows, columns = terms.shape
    grad = jax.ShapeDtypeStruct((blocks, rows, columns // 2), jnp.bfloat16)
    dma = pltpu.SemaphoreType.DMA
    return pl.pallas_call(
        return_kernel,
        out_shape=(jax.ShapeDtypeStruct((PLANE,) + block, jnp.bfloat16), grad, grad),
        in_specs=[pl.BlockSpec(memory_space=pltpu.VMEM)] * 2,
        out_specs=[pl.BlockSpec(memory_space=pl.ANY)] * 3,
        scratch_shapes=[
            pltpu.VMEM((2, PLANE) + block, jnp.bfloat16),
            pltpu.VMEM((PLANE,) + block, jnp.bfloat16),
            pltpu.VMEM((blocks // 2, rows, columns), jnp.bfloat16),
            pltpu.VMEM((2, blocks // 2, rows, columns // 2), jnp.bfloat16),
            dma((PLANE,)),
            dma((PLANE,)),
            dma((2, NG)),
            dma((2, NG)),
            dma,
            dma,
            dma((2, 2)),
            dma((2, 2)),
            dma((2,)),
        ],
        compiler_params=pltpu.CompilerParams(
            collective_id=1, has_side_effects=True, vmem_limit_bytes=40 << 20
        ),
    )(part, terms)


def slot_tables(expert_ids, gate_values, flight_count, capacity):
    experts = jnp.arange(flight_count, dtype=jnp.int32)
    match = (expert_ids[:, :, None] == experts[None, None, :]).astype(jnp.float32)
    counted = jnp.sum(match, axis=1)
    before = jnp.cumsum(counted, axis=0) - counted
    places = jnp.arange(capacity, dtype=jnp.float32)
    slot_hit = counted[:, :, None] * (before[:, :, None] == places[None, None, :]).astype(
        jnp.float32
    )
    gate_each = jnp.sum(match * gate_values.astype(jnp.float32)[:, :, None], axis=1)
    return (match, slot_hit, gate_each)


def per_device(tokens, expert_ids, gate_values, cotangent, w_gate, w_up, w_down):
    device_count = lax.axis_size("expert")
    hidden_dev = w_gate.shape[1]
    slice_count = FFW // hidden_dev
    flight_count = device_count // slice_count
    width = tokens.shape[1]
    capacity = CAP
    f32, bf16 = jnp.float32, jnp.bfloat16
    row_contract = (((0,), (0,)), ((), ()))
    match, slot_hit, gate_each = slot_tables(expert_ids, gate_values, flight_count, capacity)
    hit_flat = slot_hit.reshape(slot_hit.shape[0], flight_count * capacity).astype(bf16)
    token_buf = lax.dot_general(hit_flat, tokens, row_contract, preferred_element_type=f32)
    cot_buf = lax.dot_general(hit_flat, cotangent, row_contract, preferred_element_type=f32)
    gate_buf = jnp.sum(slot_hit * gate_each[:, :, None], axis=0).reshape(-1, 1)

    def to_blocks(rows):
        return rows.astype(bf16).reshape(flight_count, capacity, width)

    recv_x, recv_c = dispatch(to_blocks(token_buf), to_blocks(gate_buf * cot_buf))
    token_rows, scaled = recv_x.reshape(-1, width), recv_c.reshape(-1, width)
    pre_gate = jnp.dot(token_rows, w_gate, preferred_element_type=f32)
    pre_up = jnp.dot(token_rows, w_up, preferred_element_type=f32)
    sigmoid_gate = jax.nn.sigmoid(pre_gate)
    hidden = (pre_gate * sigmoid_gate * pre_up).astype(bf16)
    partial_out = jnp.dot(hidden, w_down, preferred_element_type=f32).astype(bf16)
    partial_out = partial_out.reshape(device_count, capacity, width)
    back_hidden = lax.dot_general(
        scaled, w_down, (((1,), (1,)), ((), ())), preferred_element_type=f32
    )
    d_up = (back_hidden * pre_gate * sigmoid_gate).astype(bf16)
    d_pre = (back_hidden * pre_up * sigmoid_gate * (1.0 + pre_gate * (1.0 - sigmoid_gate))).astype(
        bf16
    )
    terms = lax.dot_general(
        token_rows,
        jnp.concatenate([d_pre, d_up], axis=1),
        row_contract,
        preferred_element_type=f32,
    ).astype(bf16)
    returned, grad_gate, grad_up = give_back(partial_out, terms.reshape(-1, capacity, 2 * hidden_dev))

    copies = PLANE // flight_count
    weight_hit = (slot_hit * gate_each[:, :, None]).astype(bf16)
    weight_hit = jnp.repeat(weight_hit, copies, axis=1).reshape(tokens.shape[0], -1)
    mixed = jnp.dot(
        weight_hit, returned.reshape(-1, width), preferred_element_type=f32
    ).astype(bf16)
    returned = returned.reshape(flight_count, copies, capacity, width).astype(f32)
    cots = cot_buf.reshape(flight_count, 1, capacity, width)
    values = jnp.sum(returned * cots, axis=(1, 3))
    value_each = jnp.einsum("tec,ec->te", slot_hit, values, precision=lax.Precision.HIGHEST)
    gate_grad = jnp.einsum("tke,te->tk", match, value_each, precision=lax.Precision.HIGHEST)
    grad_shape = (1, width, hidden_dev)
    return (mixed, gate_grad, grad_gate.reshape(grad_shape), grad_up.reshape(grad_shape))


def solution(mesh):
    placed = (
        P(("pipe", "expert"), None),
        P(("pipe", "expert"), None),
        P(("pipe", "expert"), None),
        P(("pipe", "expert"), None),
        P(None, "expert"),
        P(None, "expert"),
        P("expert", None),
    )
    return jax.shard_map(
        per_device,
        mesh=mesh,
        in_specs=placed,
        out_specs=(
            P(("pipe", "expert"), None),
            P(("pipe", "expert"), None),
            P("pipe", None, "expert"),
            P("pipe", None, "expert"),
        ),
        check_vma=False,
    )
```

time: 408 us -> 214 us (0.52)
  waiting for transfers between devices: 250 us -> 0 us
  Pallas kernels: 0 us -> 189 us
  blocking collectives: 99.8 us -> 0 us
  starting transfers between devices: 26.7 us -> 0 us
  other arithmetic: 8.65 us -> 3.04 us
  matrix products: 15.9 us -> 11.8 us
    pallas_call x0 -> x2, Pallas kernels: none -> 189 us  [the longest x1 104 us: dispatch(): pl.pallas_call(dispatch_kernel, out_shape=(landed, landed), in_specs=[pl....]
    all_to_all x3 -> x0, waiting for transfers between devices: 172 us -> none  [the longest x1 83.3 us: per_device(): lax.all_to_all(send_cots, 'expert', split_axis=0, concat_axis=0, tiled=True)]
    all_to_all x1 -> x0, blocking collectives: 99.8 us -> none  [per_device(): lax.all_to_all(send_tokens, 'expert', split_axis=0, concat_axis=0, tiled=...]
    ppermute x4 -> x0, waiting for transfers between devices: 77.8 us -> none  [from_partner(): lax.ppermute(shard, axis, [(i, i ^ 1 << stride) for i in range(lax.axis_s...]
    all_to_all x3 -> x0, starting transfers between devices: 21.8 us -> none  [the longest x1 8.52 us: per_device(): lax.all_to_all(send_gates, 'expert', split_axis=0, concat_axis=0, tiled=T...]
    unnamed x20 -> x22, local copies, waits for them, and re-layouts: 2.54 us -> 7.79 us
    ppermute x4 -> x0, starting transfers between devices: 4.86 us -> none  [from_partner(): lax.ppermute(shard, axis, [(i, i ^ 1 << stride) for i in range(lax.axis_s...]
    dot_general x8 -> x7, matrix products: 11 us -> 9.17 us  [the longest x1 2.86 us: per_device(): jnp.dot(weight_hit, returned.reshape(-1, width), preferred_element_type=f32)]
  transfers between devices with their start and end apart: 7 -> 0, of which waited for: 7 -> 0; matrix products, arithmetic and copies ran while one was open for 3% -> 0% of each run, Pallas kernels for 0% -> 0%
where the time goes in v1:
time: 214 us; the launch traced here: 213 us
  Pallas kernels  189 us (88%)
  matrix products  11.8 us (6%)
  local copies, waits for them, and re-layouts  8.54 us (4%)
  other arithmetic  3.04 us (1%)
    pallas_call x1, Pallas kernels, dispatch(): pl.pallas_call(dispatch_kernel, out_shape=(landed, landed), in_specs=[pl....  104 us
    pallas_call x1, Pallas kernels, give_back(): pl.pallas_call(return_kernel, out_shape=(jax.ShapeDtypeStruct((PLANE,) +...  85.4 us
    unnamed x22, local copies, waits for them, and re-layouts  7.79 us

profile of v1, /device:TPU:1, one launch (start us, length us, event | category | flops | bytes accessed | tf_op | source)
XLA Modules:
  0.0 213.3 jit_solution(9639034120281443915)
XLA Ops:
  0.6 0.0 copy-start
  0.6 0.8 convert_element_type.42
  1.5 0.7 convert_reduce_fusion
  2.2 0.1 copy.21
  2.3 0.2 reduce_window_sum.11
  2.5 0.1 eq.45
  2.6 1.5 fusion.24
  4.1 0.1 fusion.20
  4.2 0.1 mul.87
  4.3 0.0 copy-start.6
  4.3 0.1 fusion.16.send_c
  4.4 1.1 copy-done.6
  5.5 0.3 fusion.1.send_x
  5.8 103.7 %shard_map.102 = (bf16[64,8,3584]{2,1,0:T(8,128)(2,1)S(1)}, bf16[64,8,3584]{2,1,0:T(8,128)(2,1)S(1)}) custom-call(bf16[8,8,3584]{2,1,0:T(8,128)(2,1)S(1)} %fusion.1.send_x, bf16[8,8,3584]{2,1,0:T(8,128)(2,1)S(1)} %fusion.16.send_c), custom_call_target="tpu_custom_call" | custom-call | tf_op jit(solution)/shard_map/pallas_call | solution.py:367
  109.5 0.0 copy-done
  109.5 0.0 copy-start.8
  109.5 1.1 fusion.2
  110.7 0.3 copy-done.8
  111.0 0.0 copy-start.9
  111.0 1.2 fusion.5
  112.2 0.3 copy-done.9
  112.5 1.3 multiply_convert_fusion.2
  113.9 2.1 fusion.9.terms
  116.0 1.2 fusion.part
  117.2 85.4 %shard_map.103 = (bf16[32,8,3584]{2,1,0:T(8,128)(2,1)S(1)}, bf16[448,8,256]{2,1,0:T(8,128)(2,1)S(1)}, bf16[448,8,256]{2,1,0:T(8,128)(2,1)S(1)}) custom-call(bf16[64,8,3584]{2,1,0:T(8,128)(2,1)S(1)} %fusion.part, bf16[448,8,512]{2,1,0:T(8,128)(2,1)S(1)} %fusion.9.terms), custom_call_target="tpu_custom_call" | custom-call | tf_op jit(solution)/shard_map/pallas_call | solution.py:390
  202.6 0.0 copy-start.4
  202.6 1.2 copy-done.4
  203.8 0.0 copy-start.2
  203.8 0.0 copy-start.1
  203.8 0.4 mul.99
  204.2 0.8 copy-done.2
  205.1 0.6 copy-done.1
  205.7 0.0 copy-start.7
  205.7 0.5 multiply_reduce_fusion
  206.2 0.0 copy-start.5
  206.2 0.2 fusion.18
  206.4 0.0 copy-done.7
  206.4 0.6 select_reduce_fusion
  207.0 2.9 %convolution_convert_fusion.2 = bf16[128,3584]{1,0:T(8,128)(2,1)} fusion(bf16[128,256]{0,1:T(8,128)(2,1)S(1)} %bitcast.66, bf16[32,8,3584]{2,1,0:T(8,128)(2,1)} %copy-done.1), kind=kOutput, calls=%fused_computation.3 | convolution fusion | flops 235339776 | bytes 2818048 | tf_op jit(solution)/shard_map/dot_general | solution.py:473
  209.9 0.0 copy-done.5
  209.9 0.0 copy-start.3
  209.9 1.2 copy.36
  211.1 0.9 copy-done.3
  212.0 1.2 copy.37
  (5 shorter events, 0.1 us)
Async XLA Ops:
  0.6 108.9 %copy-start = (bf16[256,3584]{1,0:T(8,128)(2,1)S(1)}, bf16[256,3584]{1,0:T(8,128)(2,1)}, u32[]{:S(2)}) copy-start(bf16[256,3584]{1,0:T(8,128)(2,1)} %param.13) | copy-start | bytes 5505028
  4.3 1.2 copy-start.6
  109.5 1.5 copy-start.8
  111.0 1.5 copy-start.9
  202.6 1.2 copy-start.4
  203.8 1.3 copy-start.2
  203.8 1.8 copy-start.1
  205.7 0.7 copy-start.7
  206.2 3.7 %copy-start.5 = (bf16[448,8,256]{2,1,0:T(8,128)(2,1)S(1)}, bf16[448,8,256]{2,1,0:T(8,128)(2,1)}, u32[]{:S(2)}) copy-start(bf16[448,8,256]{2,1,0:T(8,128)(2,1)} %copy-done.4) | copy-start | bytes 5505028
  209.9 2.2 %copy-start.3 = (bf16[448,8,256]{2,1,0:T(8,128)(2,1)S(1)}, bf16[448,8,256]{2,1,0:T(8,128)(2,1)}, u32[]{:S(2)}) copy-start(bf16[448,8,256]{2,1,0:T(8,128)(2,1)} %copy-done.2) | copy-start | bytes 5505028

commit v2 on v0

v2 whole, which is shorter than its diff:
```python
import jax
import jax.numpy as jnp
from jax import lax
from jax.experimental import pallas as pl
from jax.experimental.pallas import tpu as pltpu
from jax.sharding import PartitionSpec as P

FFW = 2048
CAP = 8
MESH = pl.DeviceIdType.MESH
NX, NZ, NY = 4, 8, 4
PLANE = NX * NZ
PAIRS = NZ // 2
HALF = NX * PAIRS
GRP = 4
NG = PLANE // GRP
CHUNKS = 4
TILE = 256


def where_am_i():
    p, i = lax.axis_index("pipe"), lax.axis_index("expert")
    x, z, y_hi = i // (2 * NZ), (i // 2) % NZ, i % 2
    return p, x, 2 * y_hi + p // 2, z, p % 2


def device_at(x, y, z, core):
    return ((y % 2) * 2 + core, (x * NZ + z) * 2 + y // 2)


def source_of(x, z, k):
    sign = 1 - 2 * (z % 2)
    far, dx, t = k // HALF, k // PAIRS % NX, k % PAIRS
    dz = far * (t + 1) - (1 - far) * t
    return (x + NX - dx) % NX, (z + NZ + sign * dz) % NZ


def relay_of(x, z, k):
    sign = 1 - 2 * (z % 2)
    dx, t = k // PAIRS, k % PAIRS
    dz = t * (1 - 2 * (t % 2))
    return (x + dx) % NX, (z + NZ + sign * dz) % NZ


def rank_kernel(
    send_x,
    send_c,
    w_gate,
    w_up,
    w_down,
    out_rows,
    out_gate,
    out_up,
    stage,
    x_land,
    x_rows,
    c_mid,
    c_land,
    w_land,
    w_rows,
    pre,
    hidden,
    back,
    grad,
    slopes,
    parts,
    parts_in,
    sums,
    mine,
    theirs,
    total,
    x_relay,
    x_pair,
    x_y,
    c_y,
    c_relay,
    c_pair,
    w_sem,
    h_sem,
    b_sem,
    p_sem,
    s_sem,
    core_sem,
    t_sem,
):
    p, x, y, z, core = where_am_i()
    up, down, across = (y + 1) % NY, (y + NY - 1) % NY, (y + 2) % NY
    partner, beside = y + 1 - 2 * (y % 2), (y + NY - 1 + 2 * (y % 2)) % NY
    pair = z + 1 - 2 * (z % 2)
    y_hi = y // 2
    f32, bf16 = jnp.float32, jnp.bfloat16
    slots, _, rows_each, width = x_land.shape
    half = width // 2
    hid = w_gate.shape[1]
    chunk_slots = slots // CHUNKS
    chunk = chunk_slots * 2 * rows_each
    tiles = theirs.shape[0]

    def copy_to(src, dst, sems, at, to):
        return pltpu.make_async_remote_copy(
            src_ref=src,
            dst_ref=dst,
            send_sem=sems.at[(0,) + at[0]],
            recv_sem=sems.at[(1,) + at[1]],
            device_id=device_at(*to),
            device_id_type=MESH,
        )

    def loop(first, last, body):
        def step(i, carry):
            body(i)
            return carry

        lax.fori_loop(first, last, step, 0)

    barrier = pltpu.get_barrier_semaphore()

    def greet(xd, yd, zd, to_core):
        pl.semaphore_signal(
            barrier, inc=1, device_id=device_at(xd, yd, zd, to_core), device_id_type=MESH
        )

    def greet_source(k):
        xs, zs = source_of(x, z, k)
        greet(xs, y, zs, core)

    loop(1, PLANE, greet_source)
    greet(x, across, z, core)
    greet(x, y, z, 1 - core)

    @pl.when(core == 0)
    def _():
        greet(x, beside, z, 0)

    @pl.when(core == 1)
    def _():
        greet(x, up, z, 1)
        greet(x, down, z, 1)
        greet(x, partner, z, 0)

    pl.semaphore_wait(barrier, PLANE + 3)

    def x_relay_copy(k):
        xd, zd = relay_of(x, z, k)
        src = send_x.at[xd * 2 + zd // 4]
        return copy_to(src, stage.at[k], x_relay, ((k,), (k,)), (xd, y, zd, core))

    def x_own_copy():
        return pltpu.make_async_copy(send_x.at[x * 2 + z // 4], stage.at[0], x_relay.at[1, 0])

    def x_pair_copy(g):
        src = stage.at[pl.ds(g * GRP, GRP)]
        dst = stage.at[pl.ds(HALF + g * GRP, GRP)]
        return copy_to(src, dst, x_pair, ((g,), (g,)), (x, y, pair, core))

    def x_y_copy(g, way, to):
        rows = pl.ds(g * GRP, GRP)
        at = ((way, g), (y_hi, g))
        return copy_to(stage.at[rows], x_land.at[rows, y_hi], x_y, at, (x, to, z, core))

    def x_keep_copy(g):
        rows = pl.ds(g * GRP, GRP)
        return pltpu.make_async_copy(stage.at[rows], x_land.at[rows, y_hi], x_y.at[1, y_hi, g])

    def x_y_arrived(g):
        rows = pl.ds(g * GRP, GRP)
        for b in range(2):
            at = ((0, g), (b, g))
            copy_to(
                stage.at[rows], x_land.at[rows, b], x_y, at, (x, across, z, core)
            ).wait_recv()

    def x_forward(g):
        @pl.when(core == 0)
        def _():
            x_y_copy(g, 0, across).start()
            x_keep_copy(g).start()

        @pl.when(core == 1)
        def _():
            x_y_copy(g, 0, up).start()
            x_y_copy(g, 1, down).start()

    def c_y_copy(way, to):
        at = ((way,), (y_hi,))
        return copy_to(send_c.at[to // 2], c_mid.at[:, y_hi], c_y, at, (x, to, z, core))

    def c_keep_copy():
        return pltpu.make_async_copy(send_c.at[y_hi], c_mid.at[:, y_hi], c_y.at[1, y_hi])

    def c_relay_copy(k):
        xd, zd = relay_of(x, z, k)
        src = c_mid.at[xd * 2 + zd // 4]
        return copy_to(src, c_land.at[k], c_relay, ((k,), (k,)), (xd, y, zd, core))

    def c_own_copy():
        return pltpu.make_async_copy(c_mid.at[x * 2 + z // 4], c_land.at[0], c_relay.at[1, 0])

    def c_pair_copy(g):
        src = c_land.at[pl.ds(g * GRP, GRP)]
        dst = c_land.at[pl.ds(HALF + g * GRP, GRP)]
        return copy_to(src, dst, c_pair, ((g,), (g,)), (x, y, pair, core))

    blocks = w_down.shape[0]
    w_part = blocks // 2

    def w_keep_copy():
        columns = pl.ds(pl.multiple_of(y_hi * half, 128), half)
        return pltpu.make_async_copy(w_down.at[:, :, columns], w_land.at[0], w_sem.at[1, 0])

    def w_beside_copy():
        columns = pl.ds(pl.multiple_of(beside // 2 * half, 128), half)
        rows = pl.ds(core * w_part, w_part)
        src, dst = w_down.at[rows, :, columns], w_land.at[1, rows]
        return copy_to(src, dst, w_sem, ((1,), (1,)), (x, beside, z, core))

    def w_core_copy():
        rows = pl.ds(core * w_part, w_part)
        ref = w_land.at[1, rows]
        return copy_to(ref, ref, w_sem, ((2,), (2,)), (x, y, z, 1 - core))

    def h_copy(j):
        rows = pl.ds(j * chunk, chunk)
        at = ((j,), (j,))
        return copy_to(hidden.at[0, rows], hidden.at[1, rows], h_sem, at, (x, across, z, core))

    def b_copy(j):
        rows = pl.ds(j * chunk, chunk)
        at = ((j,), (j,))
        return copy_to(back.at[0, rows], back.at[1, rows], b_sem, at, (x, across, z, core))

    def p_copy(k):
        xd, zd = source_of(x, z, k)
        dst = parts_in.at[x * NZ + z]
        return copy_to(parts.at[k], dst, p_sem, ((k,), (k,)), (xd, y, zd, core))

    def p_own_copy():
        return pltpu.make_async_copy(parts.at[0], parts_in.at[x * NZ + z], p_sem.at[1, 0])

    def s_copy(way, to):
        at = ((way,), (y_hi,))
        return copy_to(sums.at[to // 2], out_rows.at[y_hi], s_sem, at, (x, to, z, core))

    def s_keep_copy():
        return pltpu.make_async_copy(sums.at[y_hi], out_rows.at[y_hi], s_sem.at[1, y_hi])

    def core_copy(i):
        at = ((i,), (i,))
        return copy_to(mine.at[i], theirs.at[i], core_sem, at, (x, y, z, 1 - core))

    outs = (out_gate, out_up)
    tile_blocks = TILE // rows_each

    def t_copy(i, w, part, to_y, to_core):
        rows = pl.ds((part * tiles + i) * tile_blocks, tile_blocks)
        at = ((w, to_core, i), (w, part, i))
        return copy_to(
            total.at[i, w], outs[w].at[rows], t_sem, at, (x, to_y, z, to_core)
        )

    def t_keep_copy(i, w):
        rows = pl.ds(i * tile_blocks, tile_blocks)
        return pltpu.make_async_copy(total.at[i, w], outs[w].at[rows], t_sem.at[1, w, 0, i])

    def flat(block):
        return block.reshape(-1, block.shape[-1])

    x_own_copy().start()
    w_keep_copy().start()
    loop(1, HALF, lambda k: x_relay_copy(k).start())

    @pl.when(core == 0)
    def _():
        c_y_copy(0, across).start()
        c_keep_copy().start()

    @pl.when(core == 1)
    def _():
        c_y_copy(0, up).start()
        c_y_copy(1, down).start()

    w_beside_copy().start()

    x_own_copy().wait()

    def x_near(g):
        loop(jnp.maximum(g * GRP, 1), g * GRP + GRP, lambda k: x_relay_copy(k).wait_recv())
        x_pair_copy(g).start()
        x_forward(g)

    loop(0, NG // 2, x_near)

    for b in range(2):
        at = ((0,), (b,))
        copy_to(
            send_c.at[0], c_mid.at[:, b], c_y, at, (x, across, z, core)
        ).wait_recv()
    c_own_copy().start()
    loop(1, HALF, lambda k: c_relay_copy(k).start())

    def x_far(g):
        x_pair_copy(g).wait_recv()
        x_forward(g + NG // 2)

    loop(0, NG // 2, x_far)

    w_beside_copy().wait_recv()
    w_core_copy().start()
    c_own_copy().wait()

    def c_near(g):
        loop(jnp.maximum(g * GRP, 1), g * GRP + GRP, lambda k: c_relay_copy(k).wait_recv())
        c_pair_copy(g).start()

    loop(0, NG // 2, c_near)

    def forward_pass(j):
        loop(j * NG // CHUNKS, (j + 1) * NG // CHUNKS, x_y_arrived)
        rows = pl.ds(j * chunk, chunk)
        block = flat(x_land[pl.ds(j * chunk_slots, chunk_slots)])
        x_rows[rows] = block
        a = jnp.dot(block, w_gate[...], preferred_element_type=f32)
        b = jnp.dot(block, w_up[...], preferred_element_type=f32)
        pre[0, rows] = a
        pre[1, rows] = b
        hidden[0, rows] = (a * jax.nn.sigmoid(a) * b).astype(bf16)
        h_copy(j).start()

    loop(0, CHUNKS, forward_pass)

    w_keep_copy().wait()
    w_core_copy().wait_recv()
    for i in range(2):
        w_rows[pl.ds(i * hid, hid)] = flat(w_land[i])

    def output_pass(j):
        h_copy(j).wait_recv()
        rows = pl.ds(j * chunk, chunk)
        both = jnp.dot(hidden[0, rows], w_rows[:hid], preferred_element_type=f32)
        both += jnp.dot(hidden[1, rows], w_rows[hid:], preferred_element_type=f32)
        both = both.reshape(chunk_slots, 2, rows_each, half).astype(bf16)
        parts[pl.ds(j * chunk_slots, chunk_slots)] = both
        first = j * chunk_slots
        loop(jnp.maximum(first, 1), first + chunk_slots, lambda k: p_copy(k).start())

    def back_pass(j):
        @pl.when(j >= CHUNKS // 2)
        def _():
            per = NG // CHUNKS
            first = j * per - NG // 2
            loop(first, first + per, lambda g: c_pair_copy(g).wait_recv())

        rows = pl.ds(j * chunk, chunk)
        block = flat(c_land[pl.ds(j * chunk_slots, chunk_slots)])
        contract = (((1,), (1,)), ((), ()))
        own = lax.dot_general(block, w_rows[:hid], contract, preferred_element_type=f32)
        other = lax.dot_general(block, w_rows[hid:], contract, preferred_element_type=f32)
        back[0, rows] = other.astype(bf16)
        b_copy(j).start()
        grad[rows] = own

    def pass_j(j):
        output_pass(j)
        back_pass(j)

    loop(0, CHUNKS, pass_j)
    p_own_copy().start()

    def grad_pass(j):
        b_copy(j).wait_recv()
        rows = pl.ds(j * chunk, chunk)
        whole = grad[rows] + back[1, rows].astype(f32)
        a, b = pre[0, rows], pre[1, rows]
        s = jax.nn.sigmoid(a)
        slopes[rows, :hid] = (whole * b * s * (1.0 + a * (1.0 - s))).astype(bf16)
        slopes[rows, hid:] = (whole * a * s).astype(bf16)

    loop(0, CHUNKS, grad_pass)

    def term(tile):
        columns = pl.ds(pl.multiple_of(tile * TILE, TILE), TILE)
        contract = (((0,), (0,)), ((), ()))
        return lax.dot_general(
            x_rows[:, columns], slopes[...], contract, preferred_element_type=f32
        )

    def term_for_other(i):
        mine[i] = term((1 - core) * tiles + i).astype(bf16)
        core_copy(i).start()

    loop(0, tiles, term_for_other)

    def term_here(i):
        own = term(core * tiles + i)
        core_copy(i).wait_recv()
        both = (own + theirs[i].astype(f32)).reshape(tile_blocks, rows_each, 2 * hid)
        total[i, 0] = both[:, :, :hid].astype(bf16)
        total[i, 1] = both[:, :, hid:].astype(bf16)

        @pl.when(core == 0)
        def _():
            for w in range(2):
                t_copy(i, w, 0, partner, 1).start()
                t_keep_copy(i, w).start()

        @pl.when(core == 1)
        def _():
            for w in range(2):
                t_copy(i, w, 1, partner, 1).start()
                t_copy(i, w, 1, y, 0).start()

    loop(0, tiles, term_here)

    p_own_copy().wait()
    loop(1, PLANE, lambda k: p_copy(k).wait_recv())
    experts = sums.shape[1]
    copies = PLANE // experts

    def sum_expert(e):
        acc = parts_in[e * copies].astype(f32)
        for i in range(1, copies):
            acc += parts_in[e * copies + i].astype(f32)
        for b in range(2):
            sums[b, e] = acc[b].astype(bf16)

    loop(0, experts, sum_expert)

    @pl.when(core == 0)
    def _():
        s_copy(0, across).start()
        s_keep_copy().start()

    @pl.when(core == 1)
    def _():
        s_copy(0, up).start()
        s_copy(1, down).start()

    loop(1, HALF, lambda k: x_relay_copy(k).wait_send())
    loop(1, HALF, lambda k: c_relay_copy(k).wait_send())
    loop(0, NG // 2, lambda g: x_pair_copy(g).wait_send())
    loop(0, NG // 2, lambda g: c_pair_copy(g).wait_send())
    loop(0, CHUNKS, lambda j: h_copy(j).wait_send())
    loop(0, CHUNKS, lambda j: b_copy(j).wait_send())
    loop(1, PLANE, lambda k: p_copy(k).wait_send())
    loop(0, tiles, lambda i: core_copy(i).wait_send())
    w_beside_copy().wait_send()
    w_core_copy().wait_send()
    for b in range(2):
        at = ((0,), (b,))
        copy_to(sums.at[0], out_rows.at[b], s_sem, at, (x, across, z, core)).wait_recv()

    @pl.when(core == 0)
    def _():
        loop(0, NG, lambda g: x_y_copy(g, 0, across).wait_send())
        c_y_copy(0, across).wait_send()
        s_copy(0, across).wait_send()

        def finish(i):
            for w in range(2):
                t_copy(i, w, 0, partner, 1).wait_send()
                t_keep_copy(i, w).wait()
                t_copy(i, w, 1, y, 0).wait_recv()

        loop(0, tiles, finish)

    @pl.when(core == 1)
    def _():
        def finish_rows(g):
            x_y_copy(g, 0, up).wait_send()
            x_y_copy(g, 1, down).wait_send()

        loop(0, NG, finish_rows)
        c_y_copy(0, up).wait_send()
        c_y_copy(1, down).wait_send()
        s_copy(0, up).wait_send()
        s_copy(1, down).wait_send()

        def finish(i):
            for w in range(2):
                t_copy(i, w, 1, partner, 1).wait()
                t_copy(i, w, 1, y, 0).wait_send()
                t_copy(i, w, 0, partner, 1).wait_recv()

        loop(0, tiles, finish)


def run_ranks(send_x, send_c, w_gate, w_up, w_down):
    experts, rows, width = send_x.shape
    hid = w_gate.shape[1]
    half, hid_blocks, all_rows = width // 2, hid // rows, 2 * PLANE * rows
    tiles = half // TILE
    bf16, f32, vmem, dma = jnp.bfloat16, jnp.float32, pltpu.VMEM, pltpu.SemaphoreType.DMA
    grad = jax.ShapeDtypeStruct((width // rows, rows, hid), bf16)
    return pl.pallas_call(
        rank_kernel,
        out_shape=(jax.ShapeDtypeStruct((2, experts, rows, half), bf16), grad, grad),
        in_specs=[pl.BlockSpec(memory_space=vmem)] * 5,
        out_specs=[pl.BlockSpec(memory_space=pl.ANY)] * 3,
        scratch_shapes=[
            vmem((PLANE, rows, width), bf16),
            vmem((PLANE, 2, rows, width), bf16),
            vmem((all_rows, width), bf16),
            vmem((experts, 2, rows, half), bf16),
            vmem((PLANE, 2, rows, half), bf16),
            vmem((2, hid_blocks, rows, half), bf16),
            vmem((2 * hid, half), bf16),
            vmem((2, all_rows, hid), f32),
            vmem((2, all_rows, hid), bf16),
            vmem((2, all_rows, hid), bf16),
            vmem((all_rows, hid), f32),
            vmem((all_rows, 2 * hid), bf16),
            vmem((PLANE, 2, rows, half), bf16),
            vmem((PLANE, 2, rows, half), bf16),
            vmem((2, experts, rows, half), bf16),
            vmem((tiles, TILE, 2 * hid), bf16),
            vmem((tiles, TILE, 2 * hid), bf16),
            vmem((tiles, 2, TILE // rows, rows, hid), bf16),
            dma((2, HALF)),
            dma((2, NG // 2)),
            dma((2, 2, NG)),
            dma((2, 2)),
            dma((2, HALF)),
            dma((2, NG // 2)),
            dma((2, 3)),
            dma((2, CHUNKS)),
            dma((2, CHUNKS)),
            dma((2, PLANE)),
            dma((2, 2)),
            dma((2, tiles)),
            dma((2, 2, 2, tiles)),
        ],
        compiler_params=pltpu.CompilerParams(
            collective_id=0, has_side_effects=True, vmem_limit_bytes=54 << 20
        ),
    )(send_x, send_c, w_gate, w_up, w_down)


def slot_tables(expert_ids, gate_values, flight_count, capacity):
    experts = jnp.arange(flight_count, dtype=jnp.int32)
    match = (expert_ids[:, :, None] == experts[None, None, :]).astype(jnp.float32)
    counted = jnp.sum(match, axis=1)
    before = jnp.cumsum(counted, axis=0) - counted
    places = jnp.arange(capacity, dtype=jnp.float32)
    slot_hit = counted[:, :, None] * (before[:, :, None] == places[None, None, :]).astype(
        jnp.float32
    )
    gate_each = jnp.sum(match * gate_values.astype(jnp.float32)[:, :, None], axis=1)
    return (match, slot_hit, gate_each)


def per_device(tokens, expert_ids, gate_values, cotangent, w_gate, w_up, w_down):
    device_count = lax.axis_size("expert")
    hidden_dev = w_gate.shape[1]
    slice_count = FFW // hidden_dev
    flight_count = device_count // slice_count
    width = tokens.shape[1]
    half = width // 2
    capacity = CAP
    f32, bf16 = jnp.float32, jnp.bfloat16
    row_contract = (((0,), (0,)), ((), ()))
    match, slot_hit, gate_each = slot_tables(expert_ids, gate_values, flight_count, capacity)
    hit_flat = slot_hit.reshape(slot_hit.shape[0], flight_count * capacity).astype(bf16)
    token_buf = lax.dot_general(hit_flat, tokens, row_contract, preferred_element_type=f32)
    cot_buf = lax.dot_general(hit_flat, cotangent, row_contract, preferred_element_type=f32)
    gate_buf = jnp.sum(slot_hit * gate_each[:, :, None], axis=0).reshape(-1, 1)
    send_x = token_buf.astype(bf16).reshape(flight_count, capacity, width)
    scaled = (gate_buf * cot_buf).astype(bf16)
    send_c = jnp.stack([scaled[:, :half], scaled[:, half:]])
    send_c = send_c.reshape(2, flight_count, capacity, half)
    w_blocks = w_down.reshape(-1, capacity, width)
    returned, grad_gate, grad_up = run_ranks(send_x, send_c, w_gate, w_up, w_blocks)

    returned = returned.reshape(2, -1, half)
    returned = jnp.concatenate([returned[0], returned[1]], axis=1)
    weight_hit = (slot_hit * gate_each[:, :, None]).astype(bf16).reshape(hit_flat.shape)
    mixed = jnp.dot(weight_hit, returned, preferred_element_type=f32).astype(bf16)
    values = jnp.sum(returned.astype(f32) * cot_buf, axis=1).reshape(flight_count, capacity)
    value_each = jnp.einsum("tec,ec->te", slot_hit, values, precision=lax.Precision.HIGHEST)
    gate_grad = jnp.einsum("tke,te->tk", match, value_each, precision=lax.Precision.HIGHEST)
    grad_shape = (1, width, hidden_dev)
    return (mixed, gate_grad, grad_gate.reshape(grad_shape), grad_up.reshape(grad_shape))


def solution(mesh):
    placed = (
        P(("pipe", "expert"), None),
        P(("pipe", "expert"), None),
        P(("pipe", "expert"), None),
        P(("pipe", "expert"), None),
        P(None, "expert"),
        P(None, "expert"),
        P("expert", None),
    )
    return jax.shard_map(
        per_device,
        mesh=mesh,
        in_specs=placed,
        out_specs=(
            P(("pipe", "expert"), None),
            P(("pipe", "expert"), None),
            P("pipe", None, "expert"),
            P("pipe", None, "expert"),
        ),
        check_vma=False,
    )
```

time: 408 us -> 156 us (0.38)
  waiting for transfers between devices: 250 us -> 0 us
  Pallas kernels: 0 us -> 142 us
  blocking collectives: 99.8 us -> 0 us
  starting transfers between devices: 26.7 us -> 0 us
  matrix products: 15.9 us -> 4.24 us
  other arithmetic: 8.65 us -> 3.35 us
    all_to_all x3 -> x0, waiting for transfers between devices: 172 us -> none  [the longest x1 83.3 us: per_device(): lax.all_to_all(send_cots, 'expert', split_axis=0, concat_axis=0, tiled=True)]
    pallas_call x0 -> x1, Pallas kernels: none -> 142 us  [run_ranks(): pl.pallas_call(rank_kernel, out_shape=(jax.ShapeDtypeStruct((2, experts,...]
    all_to_all x1 -> x0, blocking collectives: 99.8 us -> none  [per_device(): lax.all_to_all(send_tokens, 'expert', split_axis=0, concat_axis=0, tiled=...]
    ppermute x4 -> x0, waiting for transfers between devices: 77.8 us -> none  [from_partner(): lax.ppermute(shard, axis, [(i, i ^ 1 << stride) for i in range(lax.axis_s...]
    all_to_all x3 -> x0, starting transfers between devices: 21.8 us -> none  [the longest x1 8.52 us: per_device(): lax.all_to_all(send_gates, 'expert', split_axis=0, concat_axis=0, tiled=T...]
    dot_general x9 -> x3, matrix products: 14.3 us -> 3.91 us  [the longest x1 2.29 us: per_device(): lax.dot_general(hit_flat, tokens, row_contract, preferred_element_type=f32)]
    ppermute x4 -> x0, starting transfers between devices: 4.86 us -> none  [from_partner(): lax.ppermute(shard, axis, [(i, i ^ 1 << stride) for i in range(lax.axis_s...]
  transfers between devices with their start and end apart: 7 -> 0, of which waited for: 7 -> 0; matrix products, arithmetic and copies ran while one was open for 3% -> 0% of each run, Pallas kernels for 0% -> 0%
where the time goes in v2:
time: 156 us; the launch traced here: 155 us
  Pallas kernels  142 us (91%)
  local copies, waits for them, and re-layouts  5.05 us (3%)
  matrix products  4.24 us (3%)
  other arithmetic  3.35 us (2%)
    pallas_call x1, Pallas kernels, run_ranks(): pl.pallas_call(rank_kernel, out_shape=(jax.ShapeDtypeStruct((2, experts,...  142 us
    unnamed x10, local copies, waits for them, and re-layouts  3.41 us

profile of v2, /device:TPU:1, one launch (start us, length us, event | category | flops | bytes accessed | tf_op | source)
XLA Modules:
  0.0 155.4 jit_solution(14797875201336320773)
XLA Ops:
  0.6 0.0 copy-start
  0.6 0.8 convert_element_type.27
  1.4 0.7 select_reduce_fusion.1
  2.1 0.1 eq.44
  2.2 0.1 copy.15
  2.3 0.2 reduce_window_sum.11
  2.5 2.3 %fusion.send_x = bf16[8,8,3584]{2,1,0:T(8,128)(2,1)} fusion(bf16[128,3584]{1,0:T(8,128)(2,1)} %param.7, f32[128,8]{0,1:T(8,128)S(1)} %get-tuple-element.11, f32[64]{0:T(128)S(1)} %eq.44, f32[128,8]{0,1:T(8,128)S(1)} %copy.17), kind=kOutput, calls=%fused_computation.2 | convolution fusion | flops 58966016 | bytes 1384704 | tf_op jit(solution)/shard_map/dot_general | solution.py:563
  4.8 0.1 fusion.3
  4.9 0.1 mul.60
  5.0 0.0 copy-done
  5.0 0.3 multiply_convert_fusion
  5.4 0.8 pad_maximum_fusion.send_c
  6.2 142.0 %shard_map.102 = (bf16[2,8,8,1792]{3,2,1,0:T(8,128)(2,1)}, bf16[448,8,256]{2,1,0:T(8,128)(2,1)}, bf16[448,8,256]{2,1,0:T(8,128)(2,1)}) custom-call(bf16[8,8,3584]{2,1,0:T(8,128)(2,1)} %fusion.send_x, bf16[2,8,8,1792]{3,2,1,0:T(8,128)(2,1)} %pad_maximum_fusion.send_c, bf16[3584,256]{1,0:T(8,128)(2,1)} %w_gate.1, bf16[3584,256]{1,0:T(8,128)(2,1)} %w_up.1, ...), custom_call_target="tpu_custom_call" | custom-call | tf_op jit(solution)/shard_map/pallas_call | solution.py:494
  148.2 0.0 copy-start.3
  148.2 0.0 copy-start.2
  148.3 1.2 slice_bitcast_fusion.3
  149.5 1.4 convolution_convert_fusion
  150.9 0.2 multiply_reduce_fusion
  151.1 0.1 reshape.62
  151.2 0.2 fusion.1
  151.4 0.0 copy-done.3
  151.4 0.6 select_reduce_fusion
  152.0 0.0 copy-done.2
  152.0 0.0 copy-start.1
  152.0 1.2 copy.28
  153.2 0.9 copy-done.1
  154.2 1.2 copy.29
  (4 shorter events, 0.1 us)
Async XLA Ops:
  0.6 4.4 %copy-start = (bf16[128,3584]{1,0:T(8,128)(2,1)S(1)}, bf16[128,3584]{1,0:T(8,128)(2,1)}, u32[]{:S(2)}) copy-start(bf16[128,3584]{1,0:T(8,128)(2,1)} %param.10) | copy-start | bytes 2752516
  148.2 3.1 %copy-start.3 = (s32[128,8]{0,1:T(8,128)S(1)}, s32[128,8]{0,1:T(8,128)}, u32[]{:S(2)}) copy-start(s32[128,8]{0,1:T(8,128)} %param.8) | copy-start | bytes 12292
  148.2 3.7 %copy-start.2 = (bf16[448,8,256]{2,1,0:T(8,128)(2,1)S(1)}, bf16[448,8,256]{2,1,0:T(8,128)(2,1)}, u32[]{:S(2)}) copy-start(bf16[448,8,256]{2,1,0:T(8,128)(2,1)} %get-tuple-element.8) | copy-start | bytes 5505028
  152.0 2.2 %copy-start.1 = (bf16[448,8,256]{2,1,0:T(8,128)(2,1)S(1)}, bf16[448,8,256]{2,1,0:T(8,128)(2,1)}, u32[]{:S(2)}) copy-start(bf16[448,8,256]{2,1,0:T(8,128)(2,1)} %get-tuple-element.9) | copy-start | bytes 5505028

commit v3 on v2

--- a/solution.py
+++ b/solution.py
@@ -14,7 +14,7 @@
 HALF = NX * PAIRS
 GRP = 4
 NG = PLANE // GRP
-CHUNKS = 4
+CHUNKS = 2
 TILE = 256
 
 
@@ -30,14 +30,14 @@
 
 def source_of(x, z, k):
     sign = 1 - 2 * (z % 2)
-    far, dx, t = k // HALF, k // PAIRS % NX, k % PAIRS
+    far, t, dx = k // HALF, k // NX % PAIRS, k % NX
     dz = far * (t + 1) - (1 - far) * t
     return (x + NX - dx) % NX, (z + NZ + sign * dz) % NZ
 
 
 def relay_of(x, z, k):
     sign = 1 - 2 * (z % 2)
-    dx, t = k // PAIRS, k % PAIRS
+    t, dx = k // NX, k % NX
     dz = t * (1 - 2 * (t % 2))
     return (x + dx) % NX, (z + NZ + sign * dz) % NZ
 
@@ -232,17 +232,19 @@
     def p_copy(k):
         xd, zd = source_of(x, z, k)
         dst = parts_in.at[x * NZ + z]
-        return copy_to(parts.at[k], dst, p_sem, ((k,), (k,)), (xd, y, zd, core))
+        return copy_to(parts.at[k], dst, p_sem, ((k,), (x * NZ + z,)), (xd, y, zd, core))
 
     def p_own_copy():
-        return pltpu.make_async_copy(parts.at[0], parts_in.at[x * NZ + z], p_sem.at[1, 0])
-
-    def s_copy(way, to):
-        at = ((way,), (y_hi,))
-        return copy_to(sums.at[to // 2], out_rows.at[y_hi], s_sem, at, (x, to, z, core))
-
-    def s_keep_copy():
-        return pltpu.make_async_copy(sums.at[y_hi], out_rows.at[y_hi], s_sem.at[1, y_hi])
+        return pltpu.make_async_copy(
+            parts.at[0], parts_in.at[x * NZ + z], p_sem.at[1, x * NZ + z]
+        )
+
+    def s_copy(e, way, to):
+        at = ((way, e), (y_hi, e))
+        return copy_to(sums.at[to // 2, e], out_rows.at[y_hi, e], s_sem, at, (x, to, z, core))
+
+    def s_keep_copy(e):
+        return pltpu.make_async_copy(sums.at[y_hi, e], out_rows.at[y_hi, e], s_sem.at[1, y_hi, e])
 
     def core_copy(i):
         at = ((i,), (i,))
@@ -265,10 +267,6 @@
     def flat(block):
         return block.reshape(-1, block.shape[-1])
 
-    x_own_copy().start()
-    w_keep_copy().start()
-    loop(1, HALF, lambda k: x_relay_copy(k).start())
-
     @pl.when(core == 0)
     def _():
         c_y_copy(0, across).start()
@@ -279,17 +277,28 @@
         c_y_copy(0, up).start()
         c_y_copy(1, down).start()
 
+    x_own_copy().start()
+    loop(1, HALF, lambda k: x_relay_copy(k).start())
+    w_keep_copy().start()
     w_beside_copy().start()
-
-    x_own_copy().wait()
 
     def x_near(g):
         loop(jnp.maximum(g * GRP, 1), g * GRP + GRP, lambda k: x_relay_copy(k).wait_recv())
         x_pair_copy(g).start()
         x_forward(g)
 
-    loop(0, NG // 2, x_near)
-
+    def x_far(g):
+        x_pair_copy(g).wait_recv()
+        x_forward(g + NG // 2)
+
+    x_own_copy().wait()
+    x_near(0)
+
+    def x_next(g):
+        x_near(g)
+        x_far(g - 1)
+
+    loop(1, NG // 2, x_next)
     for b in range(2):
         at = ((0,), (b,))
         copy_to(
@@ -297,13 +306,7 @@
         ).wait_recv()
     c_own_copy().start()
     loop(1, HALF, lambda k: c_relay_copy(k).start())
-
-    def x_far(g):
-        x_pair_copy(g).wait_recv()
-        x_forward(g + NG // 2)
-
-    loop(0, NG // 2, x_far)
-
+    x_far(NG // 2 - 1)
     w_beside_copy().wait_recv()
     w_core_copy().start()
     c_own_copy().wait()
@@ -326,13 +329,6 @@
         hidden[0, rows] = (a * jax.nn.sigmoid(a) * b).astype(bf16)
         h_copy(j).start()
 
-    loop(0, CHUNKS, forward_pass)
-
-    w_keep_copy().wait()
-    w_core_copy().wait_recv()
-    for i in range(2):
-        w_rows[pl.ds(i * hid, hid)] = flat(w_land[i])
-
     def output_pass(j):
         h_copy(j).wait_recv()
         rows = pl.ds(j * chunk, chunk)
@@ -340,6 +336,8 @@
         both += jnp.dot(hidden[1, rows], w_rows[hid:], preferred_element_type=f32)
         both = both.reshape(chunk_slots, 2, rows_each, half).astype(bf16)
         parts[pl.ds(j * chunk_slots, chunk_slots)] = both
+
+    def send_parts(j):
         first = j * chunk_slots
         loop(jnp.maximum(first, 1), first + chunk_slots, lambda k: p_copy(k).start())
 
@@ -359,13 +357,6 @@
         b_copy(j).start()
         grad[rows] = own
 
-    def pass_j(j):
-        output_pass(j)
-        back_pass(j)
-
-    loop(0, CHUNKS, pass_j)
-    p_own_copy().start()
-
     def grad_pass(j):
         b_copy(j).wait_recv()
         rows = pl.ds(j * chunk, chunk)
@@ -375,7 +366,25 @@
         slopes[rows, :hid] = (whole * b * s * (1.0 + a * (1.0 - s))).astype(bf16)
         slopes[rows, hid:] = (whole * a * s).astype(bf16)
 
-    loop(0, CHUNKS, grad_pass)
+    def prepare_weights():
+        w_keep_copy().wait()
+        w_core_copy().wait_recv()
+        for i in range(2):
+            w_rows[pl.ds(i * hid, hid)] = flat(w_land[i])
+
+    loop(0, 1, forward_pass)
+    prepare_weights()
+    loop(0, 1, back_pass)
+    loop(1, 2, forward_pass)
+    loop(0, 1, output_pass)
+    loop(0, 1, grad_pass)
+    loop(1, 2, back_pass)
+    p_own_copy().start()
+    loop(0, 1, send_parts)
+    loop(1, 2, output_pass)
+    loop(1, 2, send_parts)
+    loop(1, 2, grad_pass)
+
 
     def term(tile):
         columns = pl.ds(pl.multiple_of(tile * TILE, TILE), TILE)
@@ -384,13 +393,9 @@
             x_rows[:, columns], slopes[...], contract, preferred_element_type=f32
         )
 
-    def term_for_other(i):
+    def term_here(i):
         mine[i] = term((1 - core) * tiles + i).astype(bf16)
         core_copy(i).start()
-
-    loop(0, tiles, term_for_other)
-
-    def term_here(i):
         own = term(core * tiles + i)
         core_copy(i).wait_recv()
         both = (own + theirs[i].astype(f32)).reshape(tile_blocks, rows_each, 2 * hid)
@@ -411,29 +416,33 @@
 
     loop(0, tiles, term_here)
 
-    p_own_copy().wait()
-    loop(1, PLANE, lambda k: p_copy(k).wait_recv())
     experts = sums.shape[1]
     copies = PLANE // experts
 
     def sum_expert(e):
+        def arrived(i):
+            copy_to(
+                parts.at[0], parts_in.at[i], p_sem, ((0,), (i,)), (x, across, z, core)
+            ).wait_recv()
+
+        loop(e * copies, e * copies + copies, arrived)
         acc = parts_in[e * copies].astype(f32)
         for i in range(1, copies):
             acc += parts_in[e * copies + i].astype(f32)
         for b in range(2):
             sums[b, e] = acc[b].astype(bf16)
 
+        @pl.when(core == 0)
+        def _():
+            s_copy(e, 0, across).start()
+            s_keep_copy(e).start()
+
+        @pl.when(core == 1)
+        def _():
+            s_copy(e, 0, up).start()
+            s_copy(e, 1, down).start()
+
     loop(0, experts, sum_expert)
-
-    @pl.when(core == 0)
-    def _():
-        s_copy(0, across).start()
-        s_keep_copy().start()
-
-    @pl.when(core == 1)
-    def _():
-        s_copy(0, up).start()
-        s_copy(1, down).start()
 
     loop(1, HALF, lambda k: x_relay_copy(k).wait_send())
     loop(1, HALF, lambda k: c_relay_copy(k).wait_send())
@@ -445,15 +454,21 @@
     loop(0, tiles, lambda i: core_copy(i).wait_send())
     w_beside_copy().wait_send()
     w_core_copy().wait_send()
-    for b in range(2):
-        at = ((0,), (b,))
-        copy_to(sums.at[0], out_rows.at[b], s_sem, at, (x, across, z, core)).wait_recv()
+
+    def s_arrived(e):
+        for b in range(2):
+            at = ((0, e), (b, e))
+            copy_to(
+                sums.at[0, e], out_rows.at[b, e], s_sem, at, (x, across, z, core)
+            ).wait_recv()
+
+    loop(0, experts, s_arrived)
 
     @pl.when(core == 0)
     def _():
         loop(0, NG, lambda g: x_y_copy(g, 0, across).wait_send())
         c_y_copy(0, across).wait_send()
-        s_copy(0, across).wait_send()
+        loop(0, experts, lambda e: s_copy(e, 0, across).wait_send())
 
         def finish(i):
             for w in range(2):
@@ -472,8 +487,8 @@
         loop(0, NG, finish_rows)
         c_y_copy(0, up).wait_send()
         c_y_copy(1, down).wait_send()
-        s_copy(0, up).wait_send()
-        s_copy(1, down).wait_send()
+        loop(0, experts, lambda e: s_copy(e, 0, up).wait_send())
+        loop(0, experts, lambda e: s_copy(e, 1, down).wait_send())
 
         def finish(i):
             for w in range(2):
@@ -525,7 +540,7 @@
             dma((2, CHUNKS)),
             dma((2, CHUNKS)),
             dma((2, PLANE)),
-            dma((2, 2)),
+            dma((2, 2, experts)),
             dma((2, tiles)),
             dma((2, 2, 2, tiles)),
         ],

time: 156 us -> 147 us (0.942)
  Pallas kernels: 142 us -> 133 us
    pallas_call x1, Pallas kernels: 142 us -> 133 us  [run_ranks(): pl.pallas_call(rank_kernel, out_shape=(jax.ShapeDtypeStruct((2, experts,...]
where the time goes in v3:
time: 147 us; the launch traced here: 146 us
  Pallas kernels  133 us (90%)
  local copies, waits for them, and re-layouts  5.05 us (3%)
  matrix products  4.24 us (3%)
  other arithmetic  3.35 us (2%)
    pallas_call x1, Pallas kernels, run_ranks(): pl.pallas_call(rank_kernel, out_shape=(jax.ShapeDtypeStruct((2, experts,...  133 us
    unnamed x10, local copies, waits for them, and re-layouts  3.41 us

profile of v3, /device:TPU:1, one launch (start us, length us, event | category | flops | bytes accessed | tf_op | source)
XLA Modules:
  0.0 146.1 jit_solution(13173694583332678331)
XLA Ops:
  0.6 0.0 copy-start
  0.6 0.8 convert_element_type.27
  1.4 0.7 select_reduce_fusion.1
  2.1 0.1 eq.44
  2.2 0.1 copy.15
  2.3 0.2 reduce_window_sum.11
  2.5 2.3 %fusion.send_x = bf16[8,8,3584]{2,1,0:T(8,128)(2,1)} fusion(bf16[128,3584]{1,0:T(8,128)(2,1)} %param.7, f32[128,8]{0,1:T(8,128)S(1)} %get-tuple-element.11, f32[64]{0:T(128)S(1)} %eq.44, f32[128,8]{0,1:T(8,128)S(1)} %copy.17), kind=kOutput, calls=%fused_computation.2 | convolution fusion | flops 58966016 | bytes 1384704 | tf_op jit(solution)/shard_map/dot_general | solution.py:578
  4.8 0.1 fusion.3
  4.9 0.1 mul.60
  5.0 0.0 copy-done
  5.0 0.3 multiply_convert_fusion
  5.4 0.8 pad_maximum_fusion.send_c
  6.2 132.8 %shard_map.102 = (bf16[2,8,8,1792]{3,2,1,0:T(8,128)(2,1)}, bf16[448,8,256]{2,1,0:T(8,128)(2,1)}, bf16[448,8,256]{2,1,0:T(8,128)(2,1)}) custom-call(bf16[8,8,3584]{2,1,0:T(8,128)(2,1)} %fusion.send_x, bf16[2,8,8,1792]{3,2,1,0:T(8,128)(2,1)} %pad_maximum_fusion.send_c, bf16[3584,256]{1,0:T(8,128)(2,1)} %w_gate.1, bf16[3584,256]{1,0:T(8,128)(2,1)} %w_up.1, ...), custom_call_target="tpu_custom_call" | custom-call | tf_op jit(solution)/shard_map/pallas_call | solution.py:509
  139.0 0.0 copy-start.3
  139.0 0.0 copy-start.2
  139.0 1.2 slice_bitcast_fusion.3
  140.2 1.4 convolution_convert_fusion
  141.6 0.2 multiply_reduce_fusion
  141.8 0.1 reshape.62
  141.9 0.2 fusion.1
  142.1 0.0 copy-done.3
  142.1 0.6 select_reduce_fusion
  142.7 0.0 copy-done.2
  142.7 0.0 copy-start.1
  142.7 1.2 copy.28
  144.0 0.9 copy-done.1
  144.9 1.2 copy.29
  (4 shorter events, 0.1 us)
Async XLA Ops:
  0.6 4.4 %copy-start = (bf16[128,3584]{1,0:T(8,128)(2,1)S(1)}, bf16[128,3584]{1,0:T(8,128)(2,1)}, u32[]{:S(2)}) copy-start(bf16[128,3584]{1,0:T(8,128)(2,1)} %param.10) | copy-start | bytes 2752516
  139.0 3.1 %copy-start.3 = (s32[128,8]{0,1:T(8,128)S(1)}, s32[128,8]{0,1:T(8,128)}, u32[]{:S(2)}) copy-start(s32[128,8]{0,1:T(8,128)} %param.8) | copy-start | bytes 12292
  139.0 3.7 %copy-start.2 = (bf16[448,8,256]{2,1,0:T(8,128)(2,1)S(1)}, bf16[448,8,256]{2,1,0:T(8,128)(2,1)}, u32[]{:S(2)}) copy-start(bf16[448,8,256]{2,1,0:T(8,128)(2,1)} %get-tuple-element.8) | copy-start | bytes 5505028
  142.7 2.2 %copy-start.1 = (bf16[448,8,256]{2,1,0:T(8,128)(2,1)S(1)}, bf16[448,8,256]{2,1,0:T(8,128)(2,1)}, u32[]{:S(2)}) copy-start(bf16[448,8,256]{2,1,0:T(8,128)(2,1)} %get-tuple-element.9) | copy-start | bytes 5505028

commit v4 on v3

--- a/solution.py
+++ b/solution.py
@@ -43,14 +43,21 @@
 
 
 def rank_kernel(
-    send_x,
-    send_c,
+    hits,
+    gates,
+    tokens,
+    cotangent,
     w_gate,
     w_up,
     w_down,
     out_rows,
     out_gate,
     out_up,
+    out_cots,
+    send_x,
+    send_c,
+    w_in,
+    w_cols,
     stage,
     x_land,
     x_rows,
@@ -76,6 +83,7 @@
     c_relay,
     c_pair,
     w_sem,
+    in_sem,
     h_sem,
     b_sem,
     p_sem,
@@ -91,7 +99,7 @@
     f32, bf16 = jnp.float32, jnp.bfloat16
     slots, _, rows_each, width = x_land.shape
     half = width // 2
-    hid = w_gate.shape[1]
+    hid = w_gate.shape[-1]
     chunk_slots = slots // CHUNKS
     chunk = chunk_slots * 2 * rows_each
     tiles = theirs.shape[0]
@@ -113,6 +121,11 @@
 
         lax.fori_loop(first, last, step, 0)
 
+    def w_load(i):
+        return pltpu.make_async_copy((w_gate, w_up)[i], w_in.at[i], in_sem.at[i])
+
+    for i in range(2):
+        w_load(i).start()
     barrier = pltpu.get_barrier_semaphore()
 
     def greet(xd, yd, zd, to_core):
@@ -137,6 +150,20 @@
         greet(x, up, z, 1)
         greet(x, down, z, 1)
         greet(x, partner, z, 0)
+
+    for c in range(width // TILE):
+        columns = slice(c * TILE, (c + 1) * TILE)
+        contract = (((0,), (0,)), ((), ()))
+        picked = lax.dot_general(
+            hits[...], tokens[:, columns], contract, preferred_element_type=f32
+        )
+        send_x[:, :, columns] = picked.reshape(-1, rows_each, TILE).astype(bf16)
+        picked = lax.dot_general(
+            hits[...], cotangent[:, columns], contract, preferred_element_type=f32
+        )
+        out_cots[:, columns] = picked.astype(bf16)
+        scaled = (gates[...] * picked).reshape(-1, rows_each, TILE).astype(bf16)
+        send_c[c // tiles, :, :, c % tiles * TILE : (c % tiles + 1) * TILE] = scaled
 
     pl.semaphore_wait(barrier, PLANE + 3)
 
@@ -239,12 +266,16 @@
             parts.at[0], parts_in.at[x * NZ + z], p_sem.at[1, x * NZ + z]
         )
 
+    own_columns = pl.ds(pl.multiple_of(y_hi * half, 128), half)
+
     def s_copy(e, way, to):
         at = ((way, e), (y_hi, e))
-        return copy_to(sums.at[to // 2, e], out_rows.at[y_hi, e], s_sem, at, (x, to, z, core))
+        dst = out_rows.at[e, :, own_columns]
+        return copy_to(sums.at[to // 2, e], dst, s_sem, at, (x, to, z, core))
 
     def s_keep_copy(e):
-        return pltpu.make_async_copy(sums.at[y_hi, e], out_rows.at[y_hi, e], s_sem.at[1, y_hi, e])
+        dst = out_rows.at[e, :, own_columns]
+        return pltpu.make_async_copy(sums.at[y_hi, e], dst, s_sem.at[1, y_hi, e])
 
     def core_copy(i):
         at = ((i,), (i,))
@@ -322,8 +353,8 @@
         rows = pl.ds(j * chunk, chunk)
         block = flat(x_land[pl.ds(j * chunk_slots, chunk_slots)])
         x_rows[rows] = block
-        a = jnp.dot(block, w_gate[...], preferred_element_type=f32)
-        b = jnp.dot(block, w_up[...], preferred_element_type=f32)
+        a = jnp.dot(block, w_cols[0], preferred_element_type=f32)
+        b = jnp.dot(block, w_cols[1], preferred_element_type=f32)
         pre[0, rows] = a
         pre[1, rows] = b
         hidden[0, rows] = (a * jax.nn.sigmoid(a) * b).astype(bf16)
@@ -371,6 +402,14 @@
         w_core_copy().wait_recv()
         for i in range(2):
             w_rows[pl.ds(i * hid, hid)] = flat(w_land[i])
+
+    for i in range(2):
+        w_load(i).wait()
+
+        def lay_out(r, i=i):
+            w_cols[i, pl.ds(r * TILE, TILE)] = flat(w_in[i, pl.ds(r * tile_blocks, tile_blocks)])
+
+        loop(0, width // TILE, lay_out)
 
     loop(0, 1, forward_pass)
     prepare_weights()
@@ -458,9 +497,8 @@
     def s_arrived(e):
         for b in range(2):
             at = ((0, e), (b, e))
-            copy_to(
-                sums.at[0, e], out_rows.at[b, e], s_sem, at, (x, across, z, core)
-            ).wait_recv()
+            dst = out_rows.at[e, :, pl.ds(b * half, half)]
+            copy_to(sums.at[0, e], dst, s_sem, at, (x, across, z, core)).wait_recv()
 
     loop(0, experts, s_arrived)
 
@@ -499,19 +537,30 @@
         loop(0, tiles, finish)
 
 
-def run_ranks(send_x, send_c, w_gate, w_up, w_down):
-    experts, rows, width = send_x.shape
-    hid = w_gate.shape[1]
+def run_ranks(hits, gates, tokens, cotangent, w_gate, w_up, w_down):
+    all_slots, width = hits.shape[1], tokens.shape[1]
+    rows, hid = w_gate.shape[1:]
+    experts = all_slots // rows
     half, hid_blocks, all_rows = width // 2, hid // rows, 2 * PLANE * rows
     tiles = half // TILE
     bf16, f32, vmem, dma = jnp.bfloat16, jnp.float32, pltpu.VMEM, pltpu.SemaphoreType.DMA
     grad = jax.ShapeDtypeStruct((width // rows, rows, hid), bf16)
+    in_vmem, anywhere = pl.BlockSpec(memory_space=vmem), pl.BlockSpec(memory_space=pl.ANY)
     return pl.pallas_call(
         rank_kernel,
-        out_shape=(jax.ShapeDtypeStruct((2, experts, rows, half), bf16), grad, grad),
-        in_specs=[pl.BlockSpec(memory_space=vmem)] * 5,
-        out_specs=[pl.BlockSpec(memory_space=pl.ANY)] * 3,
+        out_shape=(
+            jax.ShapeDtypeStruct((experts, rows, width), bf16),
+            grad,
+            grad,
+            jax.ShapeDtypeStruct((all_slots, width), bf16),
+        ),
+        in_specs=[in_vmem] * 4 + [anywhere] * 3,
+        out_specs=[anywhere] * 3 + [in_vmem],
         scratch_shapes=[
+            vmem((experts, rows, width), bf16),
+            vmem((2, experts, rows, half), bf16),
+            vmem((2, width // rows, rows, hid), bf16),
+            vmem((2, width, hid), bf16),
             vmem((PLANE, rows, width), bf16),
             vmem((PLANE, 2, rows, width), bf16),
             vmem((all_rows, width), bf16),
@@ -537,6 +586,7 @@
             dma((2, HALF)),
             dma((2, NG // 2)),
             dma((2, 3)),
+            dma((2,)),
             dma((2, CHUNKS)),
             dma((2, CHUNKS)),
             dma((2, PLANE)),
@@ -547,7 +597,7 @@
         compiler_params=pltpu.CompilerParams(
             collective_id=0, has_side_effects=True, vmem_limit_bytes=54 << 20
         ),
-    )(send_x, send_c, w_gate, w_up, w_down)
+    )(hits, gates, tokens, cotangent, w_gate, w_up, w_down)
 
 
 def slot_tables(expert_ids, gate_values, flight_count, capacity):
@@ -569,27 +619,28 @@
     slice_count = FFW // hidden_dev
     flight_count = device_count // slice_count
     width = tokens.shape[1]
-    half = width // 2
     capacity = CAP
     f32, bf16 = jnp.float32, jnp.bfloat16
-    row_contract = (((0,), (0,)), ((), ()))
     match, slot_hit, gate_each = slot_tables(expert_ids, gate_values, flight_count, capacity)
     hit_flat = slot_hit.reshape(slot_hit.shape[0], flight_count * capacity).astype(bf16)
-    token_buf = lax.dot_general(hit_flat, tokens, row_contract, preferred_element_type=f32)
-    cot_buf = lax.dot_general(hit_flat, cotangent, row_contract, preferred_element_type=f32)
     gate_buf = jnp.sum(slot_hit * gate_each[:, :, None], axis=0).reshape(-1, 1)
-    send_x = token_buf.astype(bf16).reshape(flight_count, capacity, width)
-    scaled = (gate_buf * cot_buf).astype(bf16)
-    send_c = jnp.stack([scaled[:, :half], scaled[:, half:]])
-    send_c = send_c.reshape(2, flight_count, capacity, half)
-    w_blocks = w_down.reshape(-1, capacity, width)
-    returned, grad_gate, grad_up = run_ranks(send_x, send_c, w_gate, w_up, w_blocks)
-
-    returned = returned.reshape(2, -1, half)
-    returned = jnp.concatenate([returned[0], returned[1]], axis=1)
+
+    def to_blocks(weight):
+        return weight.reshape(-1, capacity, weight.shape[1])
+
+    returned, grad_gate, grad_up, cot_buf = run_ranks(
+        hit_flat,
+        gate_buf,
+        tokens,
+        cotangent,
+        to_blocks(w_gate),
+        to_blocks(w_up),
+        to_blocks(w_down),
+    )
+    returned = returned.reshape(-1, width)
     weight_hit = (slot_hit * gate_each[:, :, None]).astype(bf16).reshape(hit_flat.shape)
     mixed = jnp.dot(weight_hit, returned, preferred_element_type=f32).astype(bf16)
-    values = jnp.sum(returned.astype(f32) * cot_buf, axis=1).reshape(flight_count, capacity)
+    values = jnp.sum(returned.astype(f32) * cot_buf.astype(f32), axis=1).reshape(flight_count, capacity)
     value_each = jnp.einsum("tec,ec->te", slot_hit, values, precision=lax.Precision.HIGHEST)
     gate_grad = jnp.einsum("tke,te->tk", match, value_each, precision=lax.Precision.HIGHEST)
     grad_shape = (1, width, hidden_dev)

time: 147 us -> 146 us (level)
  matrix products: 4.24 us -> 2.6 us
    dot_general x2 -> x0, matrix products: 2.62 us -> none  [the longest x1 2.29 us: per_device(): lax.dot_general(hit_flat, tokens, row_contract, preferred_element_type=f32)]
    unnamed x10 -> x8, local copies, waits for them, and re-layouts: 3.41 us -> 3.4 us
where the time goes in v4:
time: 146 us; the launch traced here: 145 us
  Pallas kernels  132 us (90%)
  local copies, waits for them, and re-layouts  4.62 us (3%)
  other arithmetic  4.43 us (3%)
  matrix products  2.6 us (2%)
    pallas_call x1, Pallas kernels, run_ranks(): pl.pallas_call(rank_kernel, out_shape=(jax.ShapeDtypeStruct((experts, row...  132 us
    unnamed x8, local copies, waits for them, and re-layouts  3.4 us

profile of v4, /device:TPU:1, one launch (start us, length us, event | category | flops | bytes accessed | tf_op | source)
XLA Modules:
  0.0 144.6 jit_solution(10065764515177393852)
XLA Ops:
  0.6 0.7 convert_element_type.26
  1.3 0.1 eq.45
  1.4 0.7 select_reduce_fusion.1
  2.1 0.1 copy.25
  2.2 0.1 copy.21
  2.3 0.2 reduce_window_sum.11
  2.6 0.1 fusion.4
  2.7 0.7 reshape.63.gates
  3.4 0.1 copy.24
  3.5 0.6 select_convert_fusion.hits
  4.1 0.0 copy-start.2
  4.1 132.2 %shard_map.102 = (bf16[8,8,3584]{2,1,0:T(8,128)(2,1)}, bf16[448,8,256]{2,1,0:T(8,128)(2,1)}, bf16[448,8,256]{2,1,0:T(8,128)(2,1)}, bf16[64,3584]{1,0:T(8,128)(2,1)}) custom-call(bf16[128,64]{1,0:T(8,128)(2,1)} %select_convert_fusion.hits, f32[64,1]{1,0:T(8,128)} %reshape.63.gates, bf16[128,3584]{1,0:T(8,128)(2,1)} %tokens.1, bf16[128,3584]{1,0:T(8,128)(2,1)} %cotangent.1, ...), custom_call_target="tpu_custom_call" | custom-call | tf_op jit(solution)/shard_map/pallas_call | solution.py:549
  136.4 0.0 copy-start.1
  136.4 1.5 %fusion.1 = f32[64]{0:T(128)S(1)} fusion(bf16[64,3584]{1,0:T(8,128)(2,1)} %get-tuple-element.9, bf16[8,8,3584]{2,1,0:T(8,128)(2,1)} %get-tuple-element.8), kind=kLoop, calls=%fused_computation.3 | loop fusion | flops 917440 | bytes 917760 | tf_op jit(solution)/shard_map/reduce_sum | solution.py:643
  137.9 0.1 reshape.59
  138.0 0.2 fusion.2
  138.2 0.0 copy-done.2
  138.2 0.6 select_reduce_fusion
  138.8 2.4 %fusion = bf16[128,3584]{1,0:T(8,128)(2,1)} fusion(bf16[8,8,3584]{2,1,0:T(8,128)(2,1)} %get-tuple-element.8, f32[128,8]{0,1:T(8,128)S(1)} %get-tuple-element.12, f32[128,8]{0,1:T(8,128)S(1)} %get-tuple-element.13, f32[128,8]{0,1:T(8,128)S(1)} %copy.23), kind=kOutput, calls=%fused_computation.1 | convolution fusion | flops 59211776 | bytes 1388544 | tf_op jit(solution)/shard_map/dot_general | solution.py:642
  141.2 0.0 copy-done.1
  141.2 0.0 copy-start
  141.2 1.2 copy.37
  142.4 0.9 copy-done
  143.4 1.2 copy.38
  (4 shorter events, 0.1 us)
Async XLA Ops:
  4.1 134.1 %copy-start.2 = (s32[128,8]{0,1:T(8,128)S(1)}, s32[128,8]{0,1:T(8,128)}, u32[]{:S(2)}) copy-start(s32[128,8]{0,1:T(8,128)} %param.8) | copy-start | bytes 12292
  136.4 4.8 %copy-start.1 = (bf16[448,8,256]{2,1,0:T(8,128)(2,1)S(1)}, bf16[448,8,256]{2,1,0:T(8,128)(2,1)}, u32[]{:S(2)}) copy-start(bf16[448,8,256]{2,1,0:T(8,128)(2,1)} %get-tuple-element.10) | copy-start | bytes 5505028
  141.2 2.2 %copy-start = (bf16[448,8,256]{2,1,0:T(8,128)(2,1)S(1)}, bf16[448,8,256]{2,1,0:T(8,128)(2,1)}, u32[]{:S(2)}) copy-start(bf16[448,8,256]{2,1,0:T(8,128)(2,1)} %get-tuple-element.11) | copy-start | bytes 5505028

commit v5 on v4

--- a/solution.py
+++ b/solution.py
@@ -252,7 +252,7 @@
         return copy_to(hidden.at[0, rows], hidden.at[1, rows], h_sem, at, (x, across, z, core))
 
     def b_copy(j):
-        rows = pl.ds(j * chunk, chunk)
+        rows = pl.ds(j * (chunk // 2), chunk // 2)
         at = ((j,), (j,))
         return copy_to(back.at[0, rows], back.at[1, rows], b_sem, at, (x, across, z, core))
 
@@ -382,15 +382,16 @@
         rows = pl.ds(j * chunk, chunk)
         block = flat(c_land[pl.ds(j * chunk_slots, chunk_slots)])
         contract = (((1,), (1,)), ((), ()))
-        own = lax.dot_general(block, w_rows[:hid], contract, preferred_element_type=f32)
         other = lax.dot_general(block, w_rows[hid:], contract, preferred_element_type=f32)
         back[0, rows] = other.astype(bf16)
-        b_copy(j).start()
+        b_copy(2 * j).start()
+        b_copy(2 * j + 1).start()
+        own = lax.dot_general(block, w_rows[:hid], contract, preferred_element_type=f32)
         grad[rows] = own
 
     def grad_pass(j):
         b_copy(j).wait_recv()
-        rows = pl.ds(j * chunk, chunk)
+        rows = pl.ds(j * (chunk // 2), chunk // 2)
         whole = grad[rows] + back[1, rows].astype(f32)
         a, b = pre[0, rows], pre[1, rows]
         s = jax.nn.sigmoid(a)
@@ -416,13 +417,13 @@
     loop(0, 1, back_pass)
     loop(1, 2, forward_pass)
     loop(0, 1, output_pass)
-    loop(0, 1, grad_pass)
+    loop(0, 2, grad_pass)
     loop(1, 2, back_pass)
     p_own_copy().start()
     loop(0, 1, send_parts)
     loop(1, 2, output_pass)
     loop(1, 2, send_parts)
-    loop(1, 2, grad_pass)
+    loop(2, 4, grad_pass)
 
 
     def term(tile):
@@ -488,7 +489,7 @@
     loop(0, NG // 2, lambda g: x_pair_copy(g).wait_send())
     loop(0, NG // 2, lambda g: c_pair_copy(g).wait_send())
     loop(0, CHUNKS, lambda j: h_copy(j).wait_send())
-    loop(0, CHUNKS, lambda j: b_copy(j).wait_send())
+    loop(0, 2 * CHUNKS, lambda j: b_copy(j).wait_send())
     loop(1, PLANE, lambda k: p_copy(k).wait_send())
     loop(0, tiles, lambda i: core_copy(i).wait_send())
     w_beside_copy().wait_send()
@@ -588,7 +589,7 @@
             dma((2, 3)),
             dma((2,)),
             dma((2, CHUNKS)),
-            dma((2, CHUNKS)),
+            dma((2, 2 * CHUNKS)),
             dma((2, PLANE)),
             dma((2, 2, experts)),
             dma((2, tiles)),

time: 146 us -> 146 us (level)
  no operation moved by 1% of the time
where the time goes in v5:
time: 146 us; the launch traced here: 145 us
  Pallas kernels  132 us (90%)
  local copies, waits for them, and re-layouts  4.62 us (3%)
  other arithmetic  4.43 us (3%)
  matrix products  2.59 us (2%)
    pallas_call x1, Pallas kernels, run_ranks(): pl.pallas_call(rank_kernel, out_shape=(jax.ShapeDtypeStruct((experts, row...  132 us
    unnamed x8, local copies, waits for them, and re-layouts  3.4 us

profile of v5, /device:TPU:1, one launch (start us, length us, event | category | flops | bytes accessed | tf_op | source)
XLA Modules:
  0.0 144.5 jit_solution(3866689133787598940)
XLA Ops:
  0.6 0.7 convert_element_type.26
  1.3 0.1 eq.45
  1.4 0.7 select_reduce_fusion.1
  2.1 0.1 copy.25
  2.2 0.1 copy.21
  2.3 0.2 reduce_window_sum.11
  2.6 0.1 fusion.4
  2.7 0.7 reshape.63.gates
  3.4 0.1 copy.24
  3.5 0.6 select_convert_fusion.hits
  4.1 0.0 copy-start.2
  4.1 132.2 %shard_map.102 = (bf16[8,8,3584]{2,1,0:T(8,128)(2,1)}, bf16[448,8,256]{2,1,0:T(8,128)(2,1)}, bf16[448,8,256]{2,1,0:T(8,128)(2,1)}, bf16[64,3584]{1,0:T(8,128)(2,1)}) custom-call(bf16[128,64]{1,0:T(8,128)(2,1)} %select_convert_fusion.hits, f32[64,1]{1,0:T(8,128)} %reshape.63.gates, bf16[128,3584]{1,0:T(8,128)(2,1)} %tokens.1, bf16[128,3584]{1,0:T(8,128)(2,1)} %cotangent.1, ...), custom_call_target="tpu_custom_call" | custom-call | tf_op jit(solution)/shard_map/pallas_call | solution.py:550
  136.3 0.0 copy-start.1
  136.3 1.5 %fusion.1 = f32[64]{0:T(128)S(1)} fusion(bf16[64,3584]{1,0:T(8,128)(2,1)} %get-tuple-element.9, bf16[8,8,3584]{2,1,0:T(8,128)(2,1)} %get-tuple-element.8), kind=kLoop, calls=%fused_computation.3 | loop fusion | flops 917440 | bytes 917760 | tf_op jit(solution)/shard_map/reduce_sum | solution.py:644
  137.8 0.1 reshape.59
  137.9 0.2 fusion.2
  138.1 0.0 copy-done.2
  138.1 0.6 select_reduce_fusion
  138.8 2.4 %fusion = bf16[128,3584]{1,0:T(8,128)(2,1)} fusion(bf16[8,8,3584]{2,1,0:T(8,128)(2,1)} %get-tuple-element.8, f32[128,8]{0,1:T(8,128)S(1)} %get-tuple-element.12, f32[128,8]{0,1:T(8,128)S(1)} %get-tuple-element.13, f32[128,8]{0,1:T(8,128)S(1)} %copy.23), kind=kOutput, calls=%fused_computation.1 | convolution fusion | flops 59211776 | bytes 1388544 | tf_op jit(solution)/shard_map/dot_general | solution.py:643
  141.1 0.0 copy-done.1
  141.2 0.0 copy-start
  141.2 1.2 copy.37
  142.4 0.9 copy-done
  143.3 1.2 copy.38
  (4 shorter events, 0.1 us)
Async XLA Ops:
  4.1 134.0 %copy-start.2 = (s32[128,8]{0,1:T(8,128)S(1)}, s32[128,8]{0,1:T(8,128)}, u32[]{:S(2)}) copy-start(s32[128,8]{0,1:T(8,128)} %param.8) | copy-start | bytes 12292
  136.3 4.8 %copy-start.1 = (bf16[448,8,256]{2,1,0:T(8,128)(2,1)S(1)}, bf16[448,8,256]{2,1,0:T(8,128)(2,1)}, u32[]{:S(2)}) copy-start(bf16[448,8,256]{2,1,0:T(8,128)(2,1)} %get-tuple-element.10) | copy-start | bytes 5505028
  141.2 2.2 %copy-start = (bf16[448,8,256]{2,1,0:T(8,128)(2,1)S(1)}, bf16[448,8,256]{2,1,0:T(8,128)(2,1)}, u32[]{:S(2)}) copy-start(bf16[448,8,256]{2,1,0:T(8,128)(2,1)} %get-tuple-element.11) | copy-start | bytes 5505028
